TPU v7x, 512 devices: a whole 4x8x8 slice. The times are simulated.
512 devices in a mesh: dp: 32 (over y, x_hi, core), mp: 16 (over x_lo, z).
Axes of the slice: x: 4 (x_hi: 2, x_lo: 2; x = x_hi * 2 + x_lo), y: 8, z: 8, core: 2. Of those that a mesh axis runs over, the one named last changes fastest.
Arguments:
- activations: bfloat16 [16384, 4096], P('dp'), may hold values from -6 to 6
- out_grads: bfloat16 [16384, 4096], P('dp', 'mp'), may hold values from -0.046875 to 0.046875
- input_inverse: bfloat16 [4096, 256], P('mp'), may hold values from -0.09375 to 2
- output_inverse: bfloat16 [4096, 256], P('mp'), may hold values from -0.09375 to 2
Outputs:
- preconditioned: bfloat16 [4096, 4096], P('mp', 'dp')
All inputs are finite; a program needn't handle non-finite values.
Results may differ from a plain program's by a relative error of at most 0.0058.
Values may be sent and summed in bfloat16 or wider, within the bound.
No kernel may reach another device: no remote copies, remote signals or barrier semaphores. Data moves between devices by JAX's collectives and lax.ppermute only.
A program may use at most 64 MiB of HBM per device.

v0:
```python
import jax
import jax.numpy as jnp
from jax import lax
from jax.sharding import PartitionSpec as P


def block_right(matrix, blocks):
    row_count, feature_count = matrix.shape
    block_size = blocks.shape[1]
    block_count = feature_count // block_size
    product = jnp.einsum(
        "rik,ikc->ric",
        matrix.reshape(row_count, block_count, block_size),
        blocks.reshape(block_count, block_size, block_size),
        preferred_element_type=jnp.float32,
    )
    return product.astype(jnp.bfloat16).reshape(row_count, feature_count)


def apply_outputs(output_inverse, matrix):
    row_count, feature_count = matrix.shape
    block_size = output_inverse.shape[1]
    block_count = row_count // block_size
    product = jnp.einsum(
        "jrk,jkc->jrc",
        output_inverse.reshape(block_count, block_size, block_size),
        matrix.reshape(block_count, block_size, feature_count),
        preferred_element_type=jnp.float32,
    )
    return product.astype(jnp.bfloat16).reshape(row_count, feature_count)


def apply_inputs(matrix, input_inverse):
    blocks = lax.all_gather(input_inverse, "mp", axis=0, tiled=True)
    return block_right(matrix, blocks)


def per_device(activations, out_grads, input_inverse, output_inverse):
    feature_count = activations.shape[1]
    dp_count = lax.axis_size("dp")
    col_width = feature_count // dp_count
    partial_value = lax.dot_general(
        out_grads, activations, (((0,), (0,)), ((), ())), preferred_element_type=jnp.float32
    )
    summed = lax.psum(partial_value, "dp").astype(jnp.bfloat16)
    righted = apply_inputs(summed, input_inverse)
    whole_result = apply_outputs(output_inverse, righted)
    first_col = lax.axis_index("dp") * col_width
    result = lax.dynamic_slice_in_dim(whole_result, first_col, col_width, 1)
    return result


def solution(mesh):
    in_specs = (P("dp", None), P("dp", "mp"), P("mp", None), P("mp", None))
    out_specs = P("mp", "dp")
    return jax.shard_map(
        per_device, mesh=mesh, in_specs=in_specs, out_specs=out_specs, check_vma=False
    )
```

profile of v0, /device:TPU:1, one launch (start us, length us, event | category | flops | bytes accessed | tf_op | source)
XLA Modules:
  0.0 190.6 jit_solution(2744136454419189310)
XLA Ops:
  6.5 0.0 copy-start
  6.5 0.0 all-gather.2.cloned.1.call-start
  6.5 0.7 all-gather.2.cloned.1.call-update
  7.3 0.2 copy-done
  7.5 5.4 %fusion.7 = f32[256,4096]{1,0:T(8,128)} fusion(bf16[512,256]{1,0:T(8,128)(2,1)S(1)} %copy-done, bf16[512,4096]{1,0:T(8,128)(2,1)} %param.4), kind=kOutput, calls=%fused_computation.6 | convolution fusion | flops 1073741824 | bytes 8650752 | tf_op jit(solution)/shard_map/dot_general | solution.py:42
  12.9 166.9 %all-reduce.1 = bf16[256,4096]{1,0:T(8,128)(2,1)S(1)} all-reduce(f32[256,4096]{1,0:T(8,128)} %fusion.7), channel_id=1, replica_groups=mesh['dp'=32,'mp'=16] {'dp'}, use_global_device_ids=true, to_apply=%region_0.0 | all-reduce | flops 1048576 | bytes 6291456 | tf_op jit(solution)/shard_map/psum | solution.py:45
  179.8 0.0 all-gather.2.cloned.1.call-done
  179.8 0.0 copy-start.1
  179.8 2.5 %fusion.3 = bf16[16,256,256]{1,2,0:T(8,128)(2,1)S(1)} fusion(bf16[16,256,256]{2,1,0:T(8,128)(2,1)} %bitcast.19, bf16[32,16,8,256]{3,2,1,0:T(8,128)(2,1)S(1)} %bitcast.18), kind=kOutput, calls=%fused_computation.3 | convolution fusion | flops 537919488 | bytes 6291456 | tf_op jit(solution)/shard_map/rik,ikc->ric/dot_general | solution.py:11
  182.3 0.0 copy-done.1
  182.3 0.7 fusion.8
  183.0 0.7 copy.9
  (1 shorter events, 0.0 us)
Async XLA Ops:
  6.5 1.0 copy-start
  6.5 173.2 %all-gather.2.cloned.1.call-start = ((), (), s32[]{:S(2)}) async-start(), calls=%async_computation | async-start | bytes 2228224 | tf_op jit(solution)/shard_map/all_gather | solution.py:34
  179.8 2.5 %copy-start.1 = (bf16[256,256]{1,0:T(8,128)(2,1)S(1)}, bf16[256,256]{1,0:T(8,128)(2,1)}, u32[]{:S(2)}) copy-start(bf16[256,256]{1,0:T(8,128)(2,1)} %param.7) | copy-start | bytes 393220
Sparse Core Ops, SparseCore 0:
  9.4 72.1 all-gather.1
where the time goes:
time: 191 us
  blocking collectives  167 us (87%)
  between operations  13.4 us (7%)
  matrix products  8.59 us (4%)
    psum x1, blocking collectives, per_device(): summed = lax.psum(partial_value, 'dp').astype(jnp.bfloat16)  167 us
    dot_general x1, matrix products, per_device(): lax.dot_general(out_grads, activations, (((0,), (0,)), ((), ())), preferr...  5.4 us
  transfers between devices with their start and end apart: 1, of which 0 were waited for; matrix products, arithmetic and copies ran while one was open for 3% of the time, Pallas kernels for 0%

commit v1 on v0

v1 whole, which is shorter than its diff:
```python
import functools

import jax
import jax.numpy as jnp
from jax import lax
from jax.experimental import pallas as pl
from jax.experimental.pallas import tpu as pltpu
from jax.sharding import Mesh, PartitionSpec as P

F32, BF16 = jnp.float32, jnp.bfloat16
AXES = ("y", "xh", "core", "mp")


def pairs(shape, move):
    y_n, x_n, c_n, m_n = shape

    def flat(y, x, c, m):
        return ((y * x_n + x) * c_n + c) * m_n + m

    return [
        (flat(y, x, c, m), flat(*move(y, x, c, m)))
        for y in range(y_n)
        for x in range(x_n)
        for c in range(c_n)
        for m in range(m_n)
    ]


def partial_kernel(core_ref, grads_ref, left_ref, act_ref, send_ref, keep_ref, turned):
    half, x_n = send_ref.shape[2], send_ref.shape[0]
    width = send_ref.shape[3]

    @pl.when(pl.program_id(0) == 0)
    def _():
        for part in range(2):
            first = pl.multiple_of((core_ref[0] ^ (1 - part)) * half, half)
            turned[part * half : (part + 1) * half] = lax.dot_general(
                left_ref[pl.ds(first, half)],
                grads_ref[...],
                (((1,), (1,)), ((), ())),
                preferred_element_type=F32,
            ).astype(BF16)

    product = jnp.dot(turned[...], act_ref[...], preferred_element_type=F32)
    for x in range(x_n):
        columns = slice(x * width, (x + 1) * width)
        send_ref[x, 0] = product[:half, columns].astype(BF16)
        keep_ref[x, 0] = product[half:, columns]


def partials(shape, core, activations, out_grads, output_inverse):
    y_n, x_n, c_n, _ = shape
    tokens, features = activations.shape
    rows = out_grads.shape[1]
    half, width = rows // c_n, features // (y_n * x_n)
    blocks = (x_n, y_n, half, width)
    piece = pl.BlockSpec((x_n, 1, half, width), lambda y: (0, y, 0, 0))
    return pl.pallas_call(
        partial_kernel,
        grid=(y_n,),
        out_shape=(jax.ShapeDtypeStruct(blocks, BF16), jax.ShapeDtypeStruct(blocks, F32)),
        in_specs=[
            pl.BlockSpec(memory_space=pltpu.SMEM),
            pl.BlockSpec((tokens, rows), lambda y: (0, 0)),
            pl.BlockSpec((rows, rows), lambda y: (0, 0)),
            pl.BlockSpec((tokens, x_n * width), lambda y: (0, y)),
        ],
        out_specs=(piece, piece),
        scratch_shapes=[pltpu.VMEM((rows, tokens), BF16)],
        compiler_params=pltpu.CompilerParams(vmem_limit_bytes=16 * 2**20),
    )(core.reshape(1), out_grads, output_inverse, activations)


def right_kernel(core_ref, pieces_ref, block_ref, send_ref, own_ref):
    total = pieces_ref[0].astype(F32)
    for y in range(1, pieces_ref.shape[0]):
        total += pieces_ref[y].astype(F32)
    narrow = send_ref.shape[1]
    total = total.astype(BF16)
    for ref, core in ((send_ref, 1 - core_ref[0]), (own_ref, core_ref[0])):
        first = pl.multiple_of(core * narrow, narrow)
        ref[...] = jnp.dot(
            total, block_ref[:, pl.ds(first, narrow)], preferred_element_type=F32
        ).astype(BF16)


def right(core, pieces, block):
    _, half, width = pieces.shape
    part = jax.ShapeDtypeStruct((half, width // 2), BF16)
    vmem = pl.BlockSpec(memory_space=pltpu.VMEM)
    return pl.pallas_call(
        right_kernel,
        out_shape=(part, part),
        in_specs=[pl.BlockSpec(memory_space=pltpu.SMEM), vmem, vmem],
        out_specs=(vmem, vmem),
    )(core.reshape(1), pieces, block)


def per_device(shape, activations, out_grads, input_inverse, output_inverse):
    core, xh = lax.axis_index("core"), lax.axis_index("xh")
    x_n = shape[1]

    def to_core(a):
        return lax.ppermute(a, AXES, pairs(shape, lambda y, x, c, m: (y, x, 1 - c, m)))

    def to_x(a):
        return lax.ppermute(a, AXES, pairs(shape, lambda y, x, c, m: (y, 1 - x, c, m)))

    def transpose(y, x, c, m):
        return (m // x_n, m % x_n, c, y * x_n + x)

    block = lax.ppermute(input_inverse, AXES, pairs(shape, transpose))
    send, keep = partials(shape, core, activations, out_grads, output_inverse)
    got = to_core(send)

    def summed(x):
        return lax.dynamic_index_in_dim(keep, x, 0, keepdims=False) + lax.dynamic_index_in_dim(
            got, x, 0, keepdims=False
        ).astype(F32)

    total = (summed(xh) + to_x(summed(1 - xh).astype(BF16)).astype(F32)).astype(BF16)
    pieces = lax.all_to_all(total, "y", 0, 0)
    send, own = right(core, pieces, block)
    other = to_core(send)
    return jnp.where(
        core == 0, jnp.concatenate([own, other], 0), jnp.concatenate([other, own], 0)
    )


def solution(mesh):
    dp_count, mp_count = mesh.devices.shape
    shape = (dp_count // 4, 2, 2, mp_count)
    split = Mesh(mesh.devices.reshape(shape), AXES)
    dp = AXES[:3]
    in_specs = (P(dp, None), P(dp, "mp"), P("mp", None), P("mp", None))
    return jax.shard_map(
        functools.partial(per_device, shape),
        mesh=split,
        in_specs=in_specs,
        out_specs=P("mp", dp),
        check_vma=False,
    )
```

time: 191 us -> 90.7 us (0.47)
  the two profiles are of different devices: /device:TPU:1 before, /device:TPU:51 now
where the time goes in v1:
time: 90.7 us; the launch traced here: 90.2 us
  waiting for transfers between devices  45.7 us (50%)
  starting transfers between devices  29 us (32%)
  local copies, waits for them, and re-layouts  5.48 us (6%)
  Pallas kernels  5.17 us (6%)
  other arithmetic  4.7 us (5%)
    ppermute x1, waiting for transfers between devices, per_device(): block = lax.ppermute(input_inverse, AXES, pairs(shape, transpose))  29.5 us
    ppermute x1, waiting for transfers between devices, to_x(): lax.ppermute(a, AXES, pairs(shape, lambda y, x, c, m: (y, 1 - x, c, m)))  12.8 us
    ppermute x1, starting transfers between devices, per_device(): block = lax.ppermute(input_inverse, AXES, pairs(shape, transpose))  12.4 us
    all_to_all x1, starting transfers between devices, per_device(): pieces = lax.all_to_all(total, 'y', 0, 0)  6.42 us
    ppermute x2, starting transfers between devices, to_core(): lax.ppermute(a, AXES, pairs(shape, lambda y, x, c, m: (y, x, 1 - c, m)))  6.32 us
    unnamed x12, local copies, waits for them, and re-layouts  5.48 us
    ppermute x1, starting transfers between devices, to_x(): lax.ppermute(a, AXES, pairs(shape, lambda y, x, c, m: (y, 1 - x, c, m)))  3.88 us
    ppermute x2, waiting for transfers between devices, to_core(): lax.ppermute(a, AXES, pairs(shape, lambda y, x, c, m: (y, x, 1 - c, m)))  3.43 us
  transfers between devices with their start and end apart: 5, of which 4 were waited for; matrix products, arithmetic and copies ran while one was open for 0% of the time, Pallas kernels for 0%

profile of v1, /device:TPU:51, one launch (start us, length us, event | category | flops | bytes accessed | tf_op | source)
XLA Modules:
  0.0 90.2 jit_solution(5148712609857451530)
XLA Ops:
  0.0 0.0 copy-start
  0.0 2.2 %copy-done = bf16[512,4096]{1,0:T(8,128)(2,1)S(1)} copy-done((bf16[512,4096]{1,0:T(8,128)(2,1)S(1)}, bf16[512,4096]{1,0:T(8,128)(2,1)}, u32[]{:S(2)}) %copy-start) | copy-done | bytes 4194328
  2.2 0.0 copy-start.1
  2.2 0.9 %copy-done.1 = bf16[512,256]{1,0:T(8,128)(2,1)S(1)} copy-done((bf16[512,256]{1,0:T(8,128)(2,1)S(1)}, bf16[512,256]{1,0:T(8,128)(2,1)}, u32[]{:S(2)}) %copy-start.1) | copy-done | bytes 262168
  3.1 0.0 copy-start.2
  3.1 0.9 %copy-done.2 = bf16[256,256]{1,0:T(8,128)(2,1)S(1)} copy-done((bf16[256,256]{1,0:T(8,128)(2,1)S(1)}, bf16[256,256]{1,0:T(8,128)(2,1)}, u32[]{:S(2)}) %copy-start.2) | copy-done | bytes 131096
  4.0 3.3 %shard_map.46 = (bf16[2,8,128,256]{3,2,1,0:T(8,128)(2,1)S(1)}, f32[2,8,128,256]{3,2,1,0:T(8,128)S(1)}) custom-call(s32[1]{0:T(128)} %bitcast.core_ref, bf16[512,256]{1,0:T(8,128)(2,1)S(1)} %copy-done.1, bf16[256,256]{1,0:T(8,128)(2,1)S(1)} %copy-done.2, bf16[512,4096]{1,0:T(8,128)(2,1)S(1)} %copy-done), custom_call_target="tpu_custom_call" | custom-call | tf_op jit(solution)/shard_map/pallas_call | solution.py:58
  7.3 2.6 %collective-permute-start = (bf16[2,8,128,256]{3,2,1,0:T(8,128)(2,1)S(1)}, bf16[2,8,128,256]{3,2,1,0:T(8,128)(2,1)}, u32[]{:S(2)}, u32[]{:S(2)}) collective-permute-start(bf16[2,8,128,256]{3,2,1,0:T(8,128)(2,1)S(1)} %get-tuple-element.10), channel_id=1, source_target_pairs={{0,16},{1,17},{2,18},{3,19},{4,20},{5,21},{6,22},{7,23},{8,24},{9,... | collective-permute-start | bytes 3145736 | tf_op jit(solution)/shard_map/ppermute | solution.py:104
  9.9 2.4 %collective-permute-done = bf16[2,8,128,256]{3,2,1,0:T(8,128)(2,1)} collective-permute-done((bf16[2,8,128,256]{3,2,1,0:T(8,128)(2,1)S(1)}, bf16[2,8,128,256]{3,2,1,0:T(8,128)(2,1)}, u32[]{:S(2)}, u32[]{:S(2)}) %collective-permute-start) | collective-permute-done | bytes 1048608 | tf_op jit(solution)/shard_map/ppermute | solution.py:104
  12.3 1.2 %fusion.1 = bf16[8,128,256]{2,1,0:T(8,128)(2,1)S(1)} fusion(f32[2,8,128,256]{3,2,1,0:T(8,128)S(1)} %get-tuple-element.9, s32[]{:T(128)S(6)} %select_n.20, bf16[2,8,128,256]{3,2,1,0:T(8,128)(2,1)} %collective-permute-done), kind=kLoop, calls=%fused_computation.3 | loop fusion | flops 786432 | bytes 2097156 | tf_op jit(solution)/shard_map/convert_element_type | solution.py:121
  13.5 0.0 copy-start.5
  13.5 3.9 %collective-permute-start.1 = (bf16[8,128,256]{2,1,0:T(8,128)(2,1)S(1)}, bf16[8,128,256]{2,1,0:T(8,128)(2,1)S(1)}, u32[]{:S(2)}, u32[]{:S(2)}) collective-permute-start(bf16[8,128,256]{2,1,0:T(8,128)(2,1)S(1)} %fusion.1), channel_id=1, source_target_pairs={{0,32},{1,33},{2,34},{3,35},{4,36},{5,37},{6,38},{7,39},{8,40},{9,... | collective-permute-start | bytes 1572872 | tf_op jit(solution)/shard_map/ppermute | solution.py:107
  17.4 12.8 %collective-permute-done.1 = bf16[8,128,256]{2,1,0:T(8,128)(2,1)S(1)} collective-permute-done((bf16[8,128,256]{2,1,0:T(8,128)(2,1)S(1)}, bf16[8,128,256]{2,1,0:T(8,128)(2,1)S(1)}, u32[]{:S(2)}, u32[]{:S(2)}) %collective-permute-start.1) | collective-permute-done | bytes 524320 | tf_op jit(solution)/shard_map/ppermute | solution.py:107
  30.2 2.1 %fusion = bf16[8,128,256]{2,1,0:T(8,128)(2,1)} fusion(bf16[8,128,256]{2,1,0:T(8,128)(2,1)S(1)} %collective-permute-done.1, f32[2,8,128,256]{3,2,1,0:T(8,128)S(1)} %get-tuple-element.9, s32[]{:T(128)S(6)} %select_n.19, bf16[2,8,128,256]{3,2,1,0:T(8,128)(2,1)} %collective-permute-done), kind=kLoop, calls=%fused_computation.1 | loop fusion | flops 1310720 | bytes 2621444 | tf_op jit(solution)/shard_map/convert_element_type | solution.py:121
  32.2 6.4 %all-to-all-start = ((bf16[8,128,256]{2,1,0:T(8,128)(2,1)}), bf16[8,128,256]{2,1,0:T(8,128)(2,1)S(1)}, u32[]{:S(2)}, u32[]{:S(2)}) async-start(bf16[8,128,256]{2,1,0:T(8,128)(2,1)} %fusion), calls=%async_computation | async-start | bytes 1048576 | tf_op jit(solution)/shard_map/all_to_all | solution.py:122
  38.7 0.0 copy-done.5
  38.7 12.4 %collective-permute-start.2 = (bf16[256,256]{1,0:T(8,128)(2,1)S(1)}, bf16[256,256]{1,0:T(8,128)(2,1)S(1)}, u32[]{:S(2)}, u32[]{:S(2)}) collective-permute-start(bf16[256,256]{1,0:T(8,128)(2,1)S(1)} %copy-done.5), channel_id=1, source_target_pairs={{0,0},{1,32},{2,64},{3,96},{4,128},{5,160},{6,192},{7,224},{8,256}... | collective-permute-start | bytes 393224 | tf_op jit(solution)/shard_map/ppermute | solution.py:112
  51.1 29.5 %collective-permute-done.2.block_ref = bf16[256,256]{1,0:T(8,128)(2,1)S(1)} collective-permute-done((bf16[256,256]{1,0:T(8,128)(2,1)S(1)}, bf16[256,256]{1,0:T(8,128)(2,1)S(1)}, u32[]{:S(2)}, u32[]{:S(2)}) %collective-permute-start.2) | collective-permute-done | bytes 131104 | tf_op jit(solution)/shard_map/ppermute | solution.py:112
  80.6 0.0 copy-start.4
  80.6 0.0 all-to-all-done.pieces_ref
  80.6 0.6 copy-done.4
  81.2 0.0 copy-start.3
  81.2 0.8 copy-done.3
  82.0 1.9 %shard_map.47 = (bf16[128,128]{1,0:T(8,128)(2,1)}, bf16[128,128]{1,0:T(8,128)(2,1)}) custom-call(s32[1]{0:T(128)} %bitcast.core_ref, bf16[8,128,256]{2,1,0:T(8,128)(2,1)} %copy-done.3, bf16[256,256]{1,0:T(8,128)(2,1)} %copy-done.4), custom_call_target="tpu_custom_call" | custom-call | tf_op jit(solution)/shard_map/pallas_call | solution.py:91
  83.9 3.7 %collective-permute-start.3 = (bf16[128,128]{1,0:T(8,128)(2,1)}, bf16[128,128]{1,0:T(8,128)(2,1)S(1)}, u32[]{:S(2)}, u32[]{:S(2)}) collective-permute-start(bf16[128,128]{1,0:T(8,128)(2,1)} %get-tuple-element.12), channel_id=1, source_target_pairs={{0,16},{1,17},{2,18},{3,19},{4,20},{5,21},{6,22},{7,23},{8,24},{9,... | collective-permute-start | bytes 98312 | tf_op jit(solution)/shard_map/ppermute | solution.py:104
  87.7 1.0 %collective-permute-done.3 = bf16[128,128]{1,0:T(8,128)(2,1)S(1)} collective-permute-done((bf16[128,128]{1,0:T(8,128)(2,1)}, bf16[128,128]{1,0:T(8,128)(2,1)S(1)}, u32[]{:S(2)}, u32[]{:S(2)}) %collective-permute-start.3) | collective-permute-done | bytes 32800 | tf_op jit(solution)/shard_map/ppermute | solution.py:104
  88.7 1.5 %maximum_select_fusion = bf16[256,128]{1,0:T(8,128)(2,1)} fusion(bf16[128,128]{1,0:T(8,128)(2,1)S(1)} %collective-permute-done.3, bf16[128,128]{1,0:T(8,128)(2,1)} %get-tuple-element.11, pred[]{:T(512)S(6)} %eq.3), kind=kLoop, calls=%fused_computation.4 | loop fusion | flops 294912 | bytes 131073 | tf_op jit(solution)/shard_map/jit(_where)/select_n | solution.py:125
Async XLA Ops:
  0.0 2.2 %copy-start = (bf16[512,4096]{1,0:T(8,128)(2,1)S(1)}, bf16[512,4096]{1,0:T(8,128)(2,1)}, u32[]{:S(2)}) copy-start(bf16[512,4096]{1,0:T(8,128)(2,1)} %act_ref.1) | copy-start | bytes 12582916
  2.2 0.9 %copy-start.1 = (bf16[512,256]{1,0:T(8,128)(2,1)S(1)}, bf16[512,256]{1,0:T(8,128)(2,1)}, u32[]{:S(2)}) copy-start(bf16[512,256]{1,0:T(8,128)(2,1)} %grads_ref.1) | copy-start | bytes 786436
  3.1 0.9 %copy-start.2 = (bf16[256,256]{1,0:T(8,128)(2,1)S(1)}, bf16[256,256]{1,0:T(8,128)(2,1)}, u32[]{:S(2)}) copy-start(bf16[256,256]{1,0:T(8,128)(2,1)} %left_ref.1) | copy-start | bytes 393220
  7.3 5.0 %collective-permute-start = (bf16[2,8,128,256]{3,2,1,0:T(8,128)(2,1)S(1)}, bf16[2,8,128,256]{3,2,1,0:T(8,128)(2,1)}, u32[]{:S(2)}, u32[]{:S(2)}) collective-permute-start(bf16[2,8,128,256]{3,2,1,0:T(8,128)(2,1)S(1)} %get-tuple-element.10), channel_id=1, source_target_pairs={{0,16},{1,17},{2,18},{3,19},{4,20},{5,21},{6,22},{7,23},{8,24},{9,... | collective-permute-start | bytes 3145736 | tf_op jit(solution)/shard_map/ppermute | solution.py:104
  13.5 25.2 %copy-start.5 = (bf16[256,256]{1,0:T(8,128)(2,1)S(1)}, bf16[256,256]{1,0:T(8,128)(2,1)}, u32[]{:S(2)}) copy-start(bf16[256,256]{1,0:T(8,128)(2,1)} %param.6) | copy-start | bytes 393220
  13.5 16.7 %collective-permute-start.1 = (bf16[8,128,256]{2,1,0:T(8,128)(2,1)S(1)}, bf16[8,128,256]{2,1,0:T(8,128)(2,1)S(1)}, u32[]{:S(2)}, u32[]{:S(2)}) collective-permute-start(bf16[8,128,256]{2,1,0:T(8,128)(2,1)S(1)} %fusion.1), channel_id=1, source_target_pairs={{0,32},{1,33},{2,34},{3,35},{4,36},{5,37},{6,38},{7,39},{8,40},{9,... | collective-permute-start | bytes 1572872 | tf_op jit(solution)/shard_map/ppermute | solution.py:107
  32.2 48.4 %all-to-all-start = ((bf16[8,128,256]{2,1,0:T(8,128)(2,1)}), bf16[8,128,256]{2,1,0:T(8,128)(2,1)S(1)}, u32[]{:S(2)}, u32[]{:S(2)}) async-start(bf16[8,128,256]{2,1,0:T(8,128)(2,1)} %fusion), calls=%async_computation | async-start | bytes 1048576 | tf_op jit(solution)/shard_map/all_to_all | solution.py:122
  38.7 41.9 %collective-permute-start.2 = (bf16[256,256]{1,0:T(8,128)(2,1)S(1)}, bf16[256,256]{1,0:T(8,128)(2,1)S(1)}, u32[]{:S(2)}, u32[]{:S(2)}) collective-permute-start(bf16[256,256]{1,0:T(8,128)(2,1)S(1)} %copy-done.5), channel_id=1, source_target_pairs={{0,0},{1,32},{2,64},{3,96},{4,128},{5,160},{6,192},{7,224},{8,256}... | collective-permute-start | bytes 393224 | tf_op jit(solution)/shard_map/ppermute | solution.py:112
  80.6 0.6 copy-start.4
  81.2 0.8 copy-start.3
  83.9 4.8 %collective-permute-start.3 = (bf16[128,128]{1,0:T(8,128)(2,1)}, bf16[128,128]{1,0:T(8,128)(2,1)S(1)}, u32[]{:S(2)}, u32[]{:S(2)}) collective-permute-start(bf16[128,128]{1,0:T(8,128)(2,1)} %get-tuple-element.12), channel_id=1, source_target_pairs={{0,16},{1,17},{2,18},{3,19},{4,20},{5,21},{6,22},{7,23},{8,24},{9,... | collective-permute-start | bytes 98312 | tf_op jit(solution)/shard_map/ppermute | solution.py:104

commit v2 on v1

v2 whole, which is shorter than its diff:
```python
import functools

import jax
import jax.numpy as jnp
from jax import lax
from jax.experimental import pallas as pl
from jax.experimental.pallas import tpu as pltpu
from jax.sharding import Mesh, PartitionSpec as P

F32, BF16 = jnp.float32, jnp.bfloat16
AXES = ("y", "xh", "core", "mp")
VMEM = pl.BlockSpec(memory_space=pltpu.VMEM)
SMEM = pl.BlockSpec(memory_space=pltpu.SMEM)


def pairs(shape, move):
    y_n, x_n, c_n, m_n = shape

    def flat(y, x, c, m):
        return ((y * x_n + x) * c_n + c) * m_n + m

    return [
        (flat(y, x, c, m), flat(*move(y, x, c, m)))
        for y in range(y_n)
        for x in range(x_n)
        for c in range(c_n)
        for m in range(m_n)
    ]


def spread(shape):
    y_n, x_n, _, m_n = shape
    z_n = m_n // 2

    def move(y, x, c, m):
        to_y, to_x = m // x_n, m % x_n
        low = (m // z_n) ^ x ^ to_x
        return to_y, to_x, c, low * z_n + (m % z_n + y - to_y + z_n // 2) % z_n

    return pairs(shape, move)


def partial_kernel(core_ref, grads_hbm, left_hbm, act_hbm, send_ref, keep_ref, grads, left, act, turned, sems):
    _, half, width = send_ref.shape
    tiles, _, columns = act.shape
    copies = [
        pltpu.make_async_copy(grads_hbm, grads, sems.at[0]),
        pltpu.make_async_copy(left_hbm, left, sems.at[1]),
    ]
    for tile in range(tiles):
        source = act_hbm.at[:, pl.ds(tile * columns, columns)]
        copies.append(pltpu.make_async_copy(source, act.at[tile], sems.at[2 + tile]))
    for copy in copies:
        copy.start()
    copies[0].wait()
    copies[1].wait()
    for part in range(2):
        first = pl.multiple_of((core_ref[0] ^ (1 - part)) * half, half)
        turned[part * half : (part + 1) * half] = lax.dot_general(
            left[pl.ds(first, half)],
            grads[...],
            (((1,), (1,)), ((), ())),
            preferred_element_type=F32,
        ).astype(BF16)
    for tile in range(tiles):
        copies[2 + tile].wait()
        product = jnp.dot(turned[...], act[tile], preferred_element_type=F32)
        for part in range(columns // width):
            piece = tile * (columns // width) + part
            block = product[:, part * width : (part + 1) * width]
            send_ref[piece] = block[:half].astype(BF16)
            keep_ref[piece] = block[half:]


def partials(shape, core, activations, out_grads, output_inverse, tiles=4):
    y_n, x_n, c_n, _ = shape
    tokens, features = activations.shape
    rows = out_grads.shape[1]
    blocks = (y_n * x_n, rows // c_n, features // (y_n * x_n))
    hbm = pl.BlockSpec(memory_space=pl.ANY)
    return pl.pallas_call(
        partial_kernel,
        out_shape=(pltpu.VMEM(blocks, BF16), pltpu.VMEM(blocks, F32)),
        in_specs=[SMEM, hbm, hbm, hbm],
        out_specs=(VMEM, VMEM),
        scratch_shapes=[
            pltpu.VMEM(out_grads.shape, BF16),
            pltpu.VMEM(output_inverse.shape, BF16),
            pltpu.VMEM((tiles, tokens, features // tiles), BF16),
            pltpu.VMEM((rows, tokens), BF16),
            pltpu.SemaphoreType.DMA((2 + tiles,)),
        ],
        compiler_params=pltpu.CompilerParams(vmem_limit_bytes=54 * 2**20),
    )(core.reshape(1), out_grads, output_inverse, activations)


def add_kernel(keep_ref, got_ref, total_ref):
    for piece in range(keep_ref.shape[0]):
        total_ref[piece] = (keep_ref[piece] + got_ref[piece].astype(F32)).astype(BF16)


def add(keep, got):
    return pl.pallas_call(
        add_kernel,
        out_shape=jax.ShapeDtypeStruct(got.shape, BF16),
        in_specs=[VMEM, VMEM],
        out_specs=VMEM,
        compiler_params=pltpu.CompilerParams(vmem_limit_bytes=16 * 2**20),
    )(keep, got)


def sum_kernel(pieces_ref, total_ref):
    total = pieces_ref[0].astype(F32)
    for piece in range(1, pieces_ref.shape[0]):
        total += pieces_ref[piece].astype(F32)
    total_ref[...] = total.astype(BF16)


def sum_pieces(pieces):
    return pl.pallas_call(
        sum_kernel,
        out_shape=jax.ShapeDtypeStruct(pieces.shape[1:], BF16),
        in_specs=[VMEM],
        out_specs=VMEM,
        compiler_params=pltpu.CompilerParams(vmem_limit_bytes=8 * 2**20),
    )(pieces)


def right_kernel(core_ref, own_ref, other_ref, block_ref, out_ref):
    half = own_ref.shape[0]
    core = core_ref[0]
    for ref, index in ((own_ref, core), (other_ref, 1 - core)):
        first = pl.multiple_of(index * half, half)
        out_ref[pl.ds(first, half)] = jnp.dot(
            ref[...], block_ref[...], preferred_element_type=F32
        ).astype(BF16)


def right(core, own, other, block):
    half, width = own.shape
    return pl.pallas_call(
        right_kernel,
        out_shape=jax.ShapeDtypeStruct((2 * half, width // 2), BF16),
        in_specs=[SMEM, VMEM, VMEM, VMEM],
        out_specs=VMEM,
        compiler_params=pltpu.CompilerParams(vmem_limit_bytes=8 * 2**20),
    )(core.reshape(1), own, other, block)


def per_device(shape, activations, out_grads, input_inverse, output_inverse):
    core = lax.axis_index("core")

    def to_core(a):
        return lax.ppermute(a, AXES, pairs(shape, lambda y, x, c, m: (y, x, 1 - c, m)))

    narrow = input_inverse.shape[1] // 2
    block = lax.dynamic_slice_in_dim(input_inverse, core * narrow, narrow, 1)
    block = lax.ppermute(block, AXES, spread(shape))
    send, keep = partials(shape, core, activations, out_grads, output_inverse)
    total = add(keep, to_core(send))
    gathered = sum_pieces(lax.all_to_all(total, ("y", "xh"), 0, 0))
    return right(core, gathered, to_core(gathered), block)


def solution(mesh):
    dp_count, mp_count = mesh.devices.shape
    shape = (dp_count // 4, 2, 2, mp_count)
    split = Mesh(mesh.devices.reshape(shape), AXES)
    dp = AXES[:3]
    in_specs = (P(dp, None), P(dp, "mp"), P("mp", None), P("mp", None))
    return jax.shard_map(
        functools.partial(per_device, shape),
        mesh=split,
        in_specs=in_specs,
        out_specs=P("mp", dp),
        check_vma=False,
    )
```

time: 90.7 us -> 59.6 us (0.66)
  the two profiles are of different devices: /device:TPU:51 before, /device:TPU:54 now
where the time goes in v2:
time: 59.6 us; the launch traced here: 59.3 us
  waiting for transfers between devices  28 us (47%)
  starting transfers between devices  25.9 us (43%)
  Pallas kernels  5.31 us (9%)
    all_to_all x1, waiting for transfers between devices, per_device(): gathered = sum_pieces(lax.all_to_all(total, ('y', 'xh'), 0, 0))  14.2 us
    ppermute x1, starting transfers between devices, per_device(): block = lax.ppermute(block, AXES, spread(shape))  12.7 us
    ppermute x1, waiting for transfers between devices, per_device(): block = lax.ppermute(block, AXES, spread(shape))  11.2 us
    all_to_all x1, starting transfers between devices, per_device(): gathered = sum_pieces(lax.all_to_all(total, ('y', 'xh'), 0, 0))  9.4 us
    ppermute x2, starting transfers between devices, to_core(): lax.ppermute(a, AXES, pairs(shape, lambda y, x, c, m: (y, x, 1 - c, m)))  3.84 us
    pallas_call x1, Pallas kernels, partials(): pl.pallas_call(partial_kernel, out_shape=(pltpu.VMEM(blocks, BF16), pltpu...  3.22 us
    ppermute x2, waiting for transfers between devices, to_core(): lax.ppermute(a, AXES, pairs(shape, lambda y, x, c, m: (y, x, 1 - c, m)))  2.63 us
  transfers between devices with their start and end apart: 4, of which 3 were waited for; matrix products, arithmetic and copies ran while one was open for 0% of the time, Pallas kernels for 0%

profile of v2, /device:TPU:54, one launch (start us, length us, event | category | flops | bytes accessed | tf_op | source)
XLA Modules:
  0.0 59.3 jit_solution(9715460405626385031)
XLA Ops:
  0.0 0.0 copy-start
  0.0 3.2 %shard_map.46 = (bf16[16,128,256]{2,1,0:T(8,128)(2,1)S(1)}, f32[16,128,256]{2,1,0:T(8,128)S(1)}) custom-call(s32[1]{0:T(128)} %bitcast.core_ref, bf16[512,256]{1,0:T(8,128)(2,1)} %grads_hbm.1, bf16[256,256]{1,0:T(8,128)(2,1)} %left_hbm.1, bf16[512,4096]{1,0:T(8,128)(2,1)} %act_hbm.1), custom_call_target="tpu_custom_call" | custom-call | tf_op jit(solution)/shard_map/pallas_call | solution.py:81
  3.2 1.9 %collective-permute-start = (bf16[16,128,256]{2,1,0:T(8,128)(2,1)S(1)}, bf16[16,128,256]{2,1,0:T(8,128)(2,1)S(1)}, u32[]{:S(2)}, u32[]{:S(2)}) collective-permute-start(bf16[16,128,256]{2,1,0:T(8,128)(2,1)S(1)} %get-tuple-element.8), channel_id=1, source_target_pairs={{0,16},{1,17},{2,18},{3,19},{4,20},{5,21},{6,22},{7,23},{8,24},{9,... | collective-permute-start | bytes 3145736 | tf_op jit(solution)/shard_map/ppermute | solution.py:154
  5.2 2.6 %collective-permute-done.got_ref = bf16[16,128,256]{2,1,0:T(8,128)(2,1)S(1)} collective-permute-done((bf16[16,128,256]{2,1,0:T(8,128)(2,1)S(1)}, bf16[16,128,256]{2,1,0:T(8,128)(2,1)S(1)}, u32[]{:S(2)}, u32[]{:S(2)}) %collective-permute-start) | collective-permute-done | bytes 1048608 | tf_op jit(solution)/shard_map/ppermute | solution.py:154
  7.8 1.1 %shard_map.47 = bf16[16,128,256]{2,1,0:T(8,128)(2,1)} custom-call(f32[16,128,256]{2,1,0:T(8,128)S(1)} %get-tuple-element.7.keep_ref, bf16[16,128,256]{2,1,0:T(8,128)(2,1)S(1)} %collective-permute-done.got_ref), custom_call_target="tpu_custom_call" | custom-call | tf_op jit(solution)/shard_map/pallas_call | solution.py:103
  8.9 9.4 %all-to-all-start = ((bf16[16,128,256]{2,1,0:T(8,128)(2,1)}), bf16[16,128,256]{2,1,0:T(8,128)(2,1)S(1)}, u32[]{:S(2)}, u32[]{:S(2)}) async-start(bf16[16,128,256]{2,1,0:T(8,128)(2,1)} %shard_map.47), calls=%async_computation | async-start | bytes 2097152 | tf_op jit(solution)/shard_map/all_to_all | solution.py:161
  18.3 0.0 copy-done
  18.4 12.7 %collective-permute-start.2 = (bf16[256,128]{1,0:T(8,128)(2,1)S(1)}, bf16[256,128]{1,0:T(8,128)(2,1)S(1)}, u32[]{:S(2)}, u32[]{:S(2)}) collective-permute-start(bf16[256,128]{1,0:T(8,128)(2,1)S(1)} %constant_dynamic-slice_fusion), channel_id=1, source_target_pairs={{0,4},{1,45},{2,69},{3,110},{4,134},{5,175},{6,199},{7,232},{8,264... | collective-permute-start | bytes 196616 | tf_op jit(solution)/shard_map/ppermute | solution.py:158
  31.1 14.2 %all-to-all-done.pieces_ref = bf16[16,128,256]{2,1,0:T(8,128)(2,1)S(1)} async-done(((bf16[16,128,256]{2,1,0:T(8,128)(2,1)}), bf16[16,128,256]{2,1,0:T(8,128)(2,1)S(1)}, u32[]{:S(2)}, u32[]{:S(2)}) %all-to-all-start) | async-done | bytes 1048608 | tf_op jit(solution)/shard_map/all_to_all | solution.py:161
  45.3 0.1 shard_map.48.own_ref
  45.4 1.9 %collective-permute-start.1 = (bf16[128,256]{1,0:T(8,128)(2,1)S(1)}, bf16[128,256]{1,0:T(8,128)(2,1)S(1)}, u32[]{:S(2)}, u32[]{:S(2)}) collective-permute-start(bf16[128,256]{1,0:T(8,128)(2,1)S(1)} %shard_map.48.own_ref), channel_id=1, source_target_pairs={{0,16},{1,17},{2,18},{3,19},{4,20},{5,21},{6,22},{7,23},{8,24},{9,... | collective-permute-start | bytes 196616 | tf_op jit(solution)/shard_map/ppermute | solution.py:154
  47.3 11.2 %collective-permute-done.2.block_ref = bf16[256,128]{1,0:T(8,128)(2,1)S(1)} collective-permute-done((bf16[256,128]{1,0:T(8,128)(2,1)S(1)}, bf16[256,128]{1,0:T(8,128)(2,1)S(1)}, u32[]{:S(2)}, u32[]{:S(2)}) %collective-permute-start.2) | collective-permute-done | bytes 65568 | tf_op jit(solution)/shard_map/ppermute | solution.py:158
  58.5 0.0 collective-permute-done.1.other_ref
  58.5 0.8 %shard_map.49 = bf16[256,128]{1,0:T(8,128)(2,1)} custom-call(s32[1]{0:T(128)} %bitcast.core_ref, bf16[128,256]{1,0:T(8,128)(2,1)S(1)} %shard_map.48.own_ref, bf16[128,256]{1,0:T(8,128)(2,1)S(1)} %collective-permute-done.1.other_ref, bf16[256,128]{1,0:T(8,128)(2,1)S(1)} %collective-permute-done.2.block_ref), custom_call_target="tpu_custom_call" | custom-call | tf_op jit(solution)/shard_map/pallas_call | solution.py:141
  (1 shorter events, 0.0 us)
Async XLA Ops:
  0.0 18.3 %copy-start = (bf16[256,256]{1,0:T(8,128)(2,1)S(1)}, bf16[256,256]{1,0:T(8,128)(2,1)}, u32[]{:S(2)}) copy-start(bf16[256,256]{1,0:T(8,128)(2,1)} %param.6) | copy-start | bytes 393220
  3.2 4.6 %collective-permute-start = (bf16[16,128,256]{2,1,0:T(8,128)(2,1)S(1)}, bf16[16,128,256]{2,1,0:T(8,128)(2,1)S(1)}, u32[]{:S(2)}, u32[]{:S(2)}) collective-permute-start(bf16[16,128,256]{2,1,0:T(8,128)(2,1)S(1)} %get-tuple-element.8), channel_id=1, source_target_pairs={{0,16},{1,17},{2,18},{3,19},{4,20},{5,21},{6,22},{7,23},{8,24},{9,... | collective-permute-start | bytes 3145736 | tf_op jit(solution)/shard_map/ppermute | solution.py:154
  8.9 36.3 %all-to-all-start = ((bf16[16,128,256]{2,1,0:T(8,128)(2,1)}), bf16[16,128,256]{2,1,0:T(8,128)(2,1)S(1)}, u32[]{:S(2)}, u32[]{:S(2)}) async-start(bf16[16,128,256]{2,1,0:T(8,128)(2,1)} %shard_map.47), calls=%async_computation | async-start | bytes 2097152 | tf_op jit(solution)/shard_map/all_to_all | solution.py:161
  18.4 40.2 %collective-permute-start.2 = (bf16[256,128]{1,0:T(8,128)(2,1)S(1)}, bf16[256,128]{1,0:T(8,128)(2,1)S(1)}, u32[]{:S(2)}, u32[]{:S(2)}) collective-permute-start(bf16[256,128]{1,0:T(8,128)(2,1)S(1)} %constant_dynamic-slice_fusion), channel_id=1, source_target_pairs={{0,4},{1,45},{2,69},{3,110},{4,134},{5,175},{6,199},{7,232},{8,264... | collective-permute-start | bytes 196616 | tf_op jit(solution)/shard_map/ppermute | solution.py:158
  45.4 13.1 %collective-permute-start.1 = (bf16[128,256]{1,0:T(8,128)(2,1)S(1)}, bf16[128,256]{1,0:T(8,128)(2,1)S(1)}, u32[]{:S(2)}, u32[]{:S(2)}) collective-permute-start(bf16[128,256]{1,0:T(8,128)(2,1)S(1)} %shard_map.48.own_ref), channel_id=1, source_target_pairs={{0,16},{1,17},{2,18},{3,19},{4,20},{5,21},{6,22},{7,23},{8,24},{9,... | collective-permute-start | bytes 196616 | tf_op jit(solution)/shard_map/ppermute | solution.py:154

commit v3 on v2

--- a/solution.py
+++ b/solution.py
@@ -37,10 +37,14 @@
         low = (m // z_n) ^ x ^ to_x
         return to_y, to_x, c, low * z_n + (m % z_n + y - to_y + z_n // 2) % z_n
 
-    return pairs(shape, move)
-
-
-def partial_kernel(core_ref, grads_hbm, left_hbm, act_hbm, send_ref, keep_ref, grads, left, act, turned, sems):
+    whole = pairs(shape, move)
+    down = [(a, b) for a, b in whole if b % z_n <= a % z_n]
+    return down, [pair for pair in whole if pair not in down]
+
+
+def partial_kernel(
+    core_ref, grads_hbm, left_hbm, right_hbm, act_hbm, send_ref, keep_ref, half_ref, grads, left, act, turned, sems
+):
     _, half, width = send_ref.shape
     tiles, _, columns = act.shape
     copies = [
@@ -50,6 +54,9 @@
     for tile in range(tiles):
         source = act_hbm.at[:, pl.ds(tile * columns, columns)]
         copies.append(pltpu.make_async_copy(source, act.at[tile], sems.at[2 + tile]))
+    narrow = half_ref.shape[1]
+    source = right_hbm.at[:, pl.ds(pl.multiple_of(core_ref[0] * narrow, narrow), narrow)]
+    copies.append(pltpu.make_async_copy(source, half_ref, sems.at[2 + tiles]))
     for copy in copies:
         copy.start()
     copies[0].wait()
@@ -70,28 +77,30 @@
             block = product[:, part * width : (part + 1) * width]
             send_ref[piece] = block[:half].astype(BF16)
             keep_ref[piece] = block[half:]
-
-
-def partials(shape, core, activations, out_grads, output_inverse, tiles=4):
+    copies[-1].wait()
+
+
+def partials(shape, core, activations, out_grads, input_inverse, output_inverse, tiles=4):
     y_n, x_n, c_n, _ = shape
     tokens, features = activations.shape
     rows = out_grads.shape[1]
+    half = (input_inverse.shape[0], input_inverse.shape[1] // c_n)
     blocks = (y_n * x_n, rows // c_n, features // (y_n * x_n))
     hbm = pl.BlockSpec(memory_space=pl.ANY)
     return pl.pallas_call(
         partial_kernel,
-        out_shape=(pltpu.VMEM(blocks, BF16), pltpu.VMEM(blocks, F32)),
-        in_specs=[SMEM, hbm, hbm, hbm],
-        out_specs=(VMEM, VMEM),
+        out_shape=(pltpu.VMEM(blocks, BF16), pltpu.VMEM(blocks, F32), pltpu.VMEM(half, BF16)),
+        in_specs=[SMEM, hbm, hbm, hbm, hbm],
+        out_specs=(VMEM, VMEM, VMEM),
         scratch_shapes=[
             pltpu.VMEM(out_grads.shape, BF16),
             pltpu.VMEM(output_inverse.shape, BF16),
             pltpu.VMEM((tiles, tokens, features // tiles), BF16),
             pltpu.VMEM((rows, tokens), BF16),
-            pltpu.SemaphoreType.DMA((2 + tiles,)),
+            pltpu.SemaphoreType.DMA((3 + tiles,)),
         ],
         compiler_params=pltpu.CompilerParams(vmem_limit_bytes=54 * 2**20),
-    )(core.reshape(1), out_grads, output_inverse, activations)
+    )(core.reshape(1), out_grads, output_inverse, input_inverse, activations)
 
 
 def add_kernel(keep_ref, got_ref, total_ref):
@@ -109,42 +118,58 @@
     )(keep, got)
 
 
-def sum_kernel(pieces_ref, total_ref):
+def sum_kernel(pieces_ref, _, total_ref):
     total = pieces_ref[0].astype(F32)
     for piece in range(1, pieces_ref.shape[0]):
         total += pieces_ref[piece].astype(F32)
     total_ref[...] = total.astype(BF16)
 
 
-def sum_pieces(pieces):
+def sum_pieces(pieces, first):
     return pl.pallas_call(
         sum_kernel,
         out_shape=jax.ShapeDtypeStruct(pieces.shape[1:], BF16),
-        in_specs=[VMEM],
+        in_specs=[VMEM, VMEM],
         out_specs=VMEM,
         compiler_params=pltpu.CompilerParams(vmem_limit_bytes=8 * 2**20),
-    )(pieces)
-
-
-def right_kernel(core_ref, own_ref, other_ref, block_ref, out_ref):
+    )(pieces, first)
+
+
+def right_kernel(core_ref, own_ref, other_ref, near_ref, far_ref, out_ref):
     half = own_ref.shape[0]
     core = core_ref[0]
+    block = near_ref[...] + far_ref[...]
     for ref, index in ((own_ref, core), (other_ref, 1 - core)):
         first = pl.multiple_of(index * half, half)
         out_ref[pl.ds(first, half)] = jnp.dot(
-            ref[...], block_ref[...], preferred_element_type=F32
+            ref[...], block, preferred_element_type=F32
         ).astype(BF16)
 
 
-def right(core, own, other, block):
+def right(core, own, other, near, far):
     half, width = own.shape
     return pl.pallas_call(
         right_kernel,
         out_shape=jax.ShapeDtypeStruct((2 * half, width // 2), BF16),
-        in_specs=[SMEM, VMEM, VMEM, VMEM],
+        in_specs=[SMEM, VMEM, VMEM, VMEM, VMEM],
         out_specs=VMEM,
         compiler_params=pltpu.CompilerParams(vmem_limit_bytes=8 * 2**20),
-    )(core.reshape(1), own, other, block)
+    )(core.reshape(1), own, other, near, far)
+
+
+def hold_kernel(block_ref, out_ref):
+    out_ref[...] = block_ref[...]
+
+
+def hold(block):
+    return pl.pallas_call(
+        hold_kernel,
+        out_shape=jax.ShapeDtypeStruct(block.shape, BF16),
+        in_specs=[VMEM],
+        out_specs=VMEM,
+        compiler_params=pltpu.CompilerParams(vmem_limit_bytes=4 * 2**20),
+        cost_estimate=pl.CostEstimate(flops=5 * 10**10, bytes_accessed=2**17, transcendentals=0),
+    )(block)
 
 
 def per_device(shape, activations, out_grads, input_inverse, output_inverse):
@@ -153,13 +178,16 @@
     def to_core(a):
         return lax.ppermute(a, AXES, pairs(shape, lambda y, x, c, m: (y, x, 1 - c, m)))
 
-    narrow = input_inverse.shape[1] // 2
-    block = lax.dynamic_slice_in_dim(input_inverse, core * narrow, narrow, 1)
-    block = lax.ppermute(block, AXES, spread(shape))
-    send, keep = partials(shape, core, activations, out_grads, output_inverse)
+    send, keep, half = partials(shape, core, activations, out_grads, input_inverse, output_inverse)
+    down, up = spread(shape)
+    near = lax.ppermute(half, AXES, down)
     total = add(keep, to_core(send))
-    gathered = sum_pieces(lax.all_to_all(total, ("y", "xh"), 0, 0))
-    return right(core, gathered, to_core(gathered), block)
+    total, half = lax.optimization_barrier((total, half))
+    far = lax.ppermute(half, AXES, up)
+    pieces = lax.all_to_all(total, ("y", "xh"), 0, 0)
+    near = hold(near)
+    gathered = sum_pieces(pieces, near)
+    return right(core, gathered, to_core(gathered), near, far)
 
 
 def solution(mesh):

time: 59.6 us -> 57 us (0.956)
  the two profiles are of different devices: /device:TPU:54 before, /device:TPU:1 now
where the time goes in v3:
time: 57 us; the launch traced here: 56.8 us
  starting transfers between devices  30.9 us (54%)
  waiting for transfers between devices  20.5 us (36%)
  Pallas kernels  5.3 us (9%)
    all_to_all x1, waiting for transfers between devices, per_device(): pieces = lax.all_to_all(total, ('y', 'xh'), 0, 0)  18.7 us
    ppermute x2, starting transfers between devices, to_core(): lax.ppermute(a, AXES, pairs(shape, lambda y, x, c, m: (y, x, 1 - c, m)))  14.9 us
    ppermute x1, starting transfers between devices, per_device(): far = lax.ppermute(half, AXES, up)  8.23 us
    all_to_all x1, starting transfers between devices, per_device(): pieces = lax.all_to_all(total, ('y', 'xh'), 0, 0)  6.42 us
    pallas_call x1, Pallas kernels, partials(): pl.pallas_call(partial_kernel, out_shape=(pltpu.VMEM(blocks, BF16), pltpu...  3.2 us
    ppermute x2, waiting for transfers between devices, to_core(): lax.ppermute(a, AXES, pairs(shape, lambda y, x, c, m: (y, x, 1 - c, m)))  1.83 us
    ppermute x1, starting transfers between devices, per_device(): near = lax.ppermute(half, AXES, down)  1.29 us
    pallas_call x1, Pallas kernels, add(): pl.pallas_call(add_kernel, out_shape=jax.ShapeDtypeStruct(got.shape, BF16...  1.14 us
  transfers between devices with their start and end apart: 5, of which 3 were waited for; matrix products, arithmetic and copies ran while one was open for 0% of the time, Pallas kernels for 2%

profile of v3, /device:TPU:1, one launch (start us, length us, event | category | flops | bytes accessed | tf_op | source)
XLA Modules:
  0.0 56.8 jit_solution(6082776548782021748)
XLA Ops:
  0.0 3.2 %shard_map.46 = (bf16[16,128,256]{2,1,0:T(8,128)(2,1)S(1)}, f32[16,128,256]{2,1,0:T(8,128)S(1)}, bf16[256,128]{1,0:T(8,128)(2,1)S(1)}) custom-call(s32[1]{0:T(128)} %bitcast.core_ref, bf16[512,256]{1,0:T(8,128)(2,1)} %grads_hbm.1, bf16[256,256]{1,0:T(8,128)(2,1)} %left_hbm.1, bf16[256,256]{1,0:T(8,128)(2,1)} %right_hbm.1, bf16[512,4096]{1,0:T(8,128)(2,1)} %act_hbm.1), custom_call_target="tpu_custom_call" | custom-call | tf_op jit(solution)/shard_map/pallas_call | solution.py:90
  3.2 8.8 %collective-permute-start = (bf16[16,128,256]{2,1,0:T(8,128)(2,1)S(1)}, bf16[16,128,256]{2,1,0:T(8,128)(2,1)S(1)}, u32[]{:S(2)}, u32[]{:S(2)}) collective-permute-start(bf16[16,128,256]{2,1,0:T(8,128)(2,1)S(1)} %get-tuple-element.11), channel_id=1, source_target_pairs={{0,16},{1,17},{2,18},{3,19},{4,20},{5,21},{6,22},{7,23},{8,24},{9,... | collective-permute-start | bytes 3145736 | tf_op jit(solution)/shard_map/ppermute | solution.py:179
  12.0 1.3 %collective-permute-start.1 = (bf16[256,128]{1,0:T(8,128)(2,1)S(1)}, bf16[256,128]{1,0:T(8,128)(2,1)S(1)}, u32[]{:S(2)}, u32[]{:S(2)}) collective-permute-start(bf16[256,128]{1,0:T(8,128)(2,1)S(1)} %get-tuple-element.14), channel_id=1, source_target_pairs={{7,232},{8,264},{9,289},{10,329},{11,354},{12,394},{13,419},{14,45... | collective-permute-start | bytes 196616 | tf_op jit(solution)/shard_map/ppermute | solution.py:183
  13.3 1.0 %collective-permute-done.got_ref = bf16[16,128,256]{2,1,0:T(8,128)(2,1)S(1)} collective-permute-done((bf16[16,128,256]{2,1,0:T(8,128)(2,1)S(1)}, bf16[16,128,256]{2,1,0:T(8,128)(2,1)S(1)}, u32[]{:S(2)}, u32[]{:S(2)}) %collective-permute-start) | collective-permute-done | bytes 1048608 | tf_op jit(solution)/shard_map/ppermute | solution.py:179
  14.3 1.1 %shard_map.47 = bf16[16,128,256]{2,1,0:T(8,128)(2,1)} custom-call(f32[16,128,256]{2,1,0:T(8,128)S(1)} %get-tuple-element.10.keep_ref, bf16[16,128,256]{2,1,0:T(8,128)(2,1)S(1)} %collective-permute-done.got_ref), custom_call_target="tpu_custom_call" | custom-call | tf_op jit(solution)/shard_map/pallas_call | solution.py:112
  15.4 6.4 %all-to-all-start = ((bf16[16,128,256]{2,1,0:T(8,128)(2,1)}), bf16[16,128,256]{2,1,0:T(8,128)(2,1)S(1)}, u32[]{:S(2)}, u32[]{:S(2)}) async-start(bf16[16,128,256]{2,1,0:T(8,128)(2,1)} %shard_map.47), calls=%async_computation | async-start | bytes 2097152 | tf_op jit(solution)/shard_map/all_to_all | solution.py:187
  21.8 0.0 collective-permute-done.1.block_ref
  21.9 8.2 %collective-permute-start.3 = (bf16[256,128]{1,0:T(8,128)(2,1)S(1)}, bf16[256,128]{1,0:T(8,128)(2,1)S(1)}, u32[]{:S(2)}, u32[]{:S(2)}) collective-permute-start(bf16[256,128]{1,0:T(8,128)(2,1)S(1)} %get-tuple-element.14), channel_id=1, source_target_pairs={{0,4},{1,45},{2,69},{3,110},{4,134},{5,175},{6,199},{16,20},{17,61... | collective-permute-start | bytes 196616 | tf_op jit(solution)/shard_map/ppermute | solution.py:186
  30.1 18.7 %all-to-all-done.pieces_ref = bf16[16,128,256]{2,1,0:T(8,128)(2,1)S(1)} async-done(((bf16[16,128,256]{2,1,0:T(8,128)(2,1)}), bf16[16,128,256]{2,1,0:T(8,128)(2,1)S(1)}, u32[]{:S(2)}, u32[]{:S(2)}) %all-to-all-start) | async-done | bytes 1048608 | tf_op jit(solution)/shard_map/all_to_all | solution.py:187
  48.8 0.1 shard_map.49.own_ref
  48.9 6.2 %collective-permute-start.2 = (bf16[128,256]{1,0:T(8,128)(2,1)S(1)}, bf16[128,256]{1,0:T(8,128)(2,1)S(1)}, u32[]{:S(2)}, u32[]{:S(2)}) collective-permute-start(bf16[128,256]{1,0:T(8,128)(2,1)S(1)} %shard_map.49.own_ref), channel_id=1, source_target_pairs={{0,16},{1,17},{2,18},{3,19},{4,20},{5,21},{6,22},{7,23},{8,24},{9,... | collective-permute-start | bytes 196616 | tf_op jit(solution)/shard_map/ppermute | solution.py:179
  55.1 0.0 collective-permute-done.3.far_ref
  55.1 0.9 %collective-permute-done.2.other_ref = bf16[128,256]{1,0:T(8,128)(2,1)S(1)} collective-permute-done((bf16[128,256]{1,0:T(8,128)(2,1)S(1)}, bf16[128,256]{1,0:T(8,128)(2,1)S(1)}, u32[]{:S(2)}, u32[]{:S(2)}) %collective-permute-start.2) | collective-permute-done | bytes 65568 | tf_op jit(solution)/shard_map/ppermute | solution.py:179
  56.0 0.8 %shard_map.50 = bf16[256,128]{1,0:T(8,128)(2,1)} custom-call(s32[1]{0:T(128)} %bitcast.core_ref, bf16[128,256]{1,0:T(8,128)(2,1)S(1)} %shard_map.49.own_ref, bf16[128,256]{1,0:T(8,128)(2,1)S(1)} %collective-permute-done.2.other_ref, bf16[256,128]{1,0:T(8,128)(2,1)S(1)} %shard_map.48._.near_ref, bf16[256,128]{1,0:T(8,128)(2,1)S(1)} %collective-permute-done.3.far_ref), custom_call_target="tpu_custom_call" | custom-call | tf_op jit(solution)/shard_map/pallas_call | solution.py:151
  (1 shorter events, 0.0 us)
Async XLA Ops:
  3.2 11.1 %collective-permute-start = (bf16[16,128,256]{2,1,0:T(8,128)(2,1)S(1)}, bf16[16,128,256]{2,1,0:T(8,128)(2,1)S(1)}, u32[]{:S(2)}, u32[]{:S(2)}) collective-permute-start(bf16[16,128,256]{2,1,0:T(8,128)(2,1)S(1)} %get-tuple-element.11), channel_id=1, source_target_pairs={{0,16},{1,17},{2,18},{3,19},{4,20},{5,21},{6,22},{7,23},{8,24},{9,... | collective-permute-start | bytes 3145736 | tf_op jit(solution)/shard_map/ppermute | solution.py:179
  12.0 9.8 %collective-permute-start.1 = (bf16[256,128]{1,0:T(8,128)(2,1)S(1)}, bf16[256,128]{1,0:T(8,128)(2,1)S(1)}, u32[]{:S(2)}, u32[]{:S(2)}) collective-permute-start(bf16[256,128]{1,0:T(8,128)(2,1)S(1)} %get-tuple-element.14), channel_id=1, source_target_pairs={{7,232},{8,264},{9,289},{10,329},{11,354},{12,394},{13,419},{14,45... | collective-permute-start | bytes 196616 | tf_op jit(solution)/shard_map/ppermute | solution.py:183
  15.4 33.4 %all-to-all-start = ((bf16[16,128,256]{2,1,0:T(8,128)(2,1)}), bf16[16,128,256]{2,1,0:T(8,128)(2,1)S(1)}, u32[]{:S(2)}, u32[]{:S(2)}) async-start(bf16[16,128,256]{2,1,0:T(8,128)(2,1)} %shard_map.47), calls=%async_computation | async-start | bytes 2097152 | tf_op jit(solution)/shard_map/all_to_all | solution.py:187
  21.9 33.2 %collective-permute-start.3 = (bf16[256,128]{1,0:T(8,128)(2,1)S(1)}, bf16[256,128]{1,0:T(8,128)(2,1)S(1)}, u32[]{:S(2)}, u32[]{:S(2)}) collective-permute-start(bf16[256,128]{1,0:T(8,128)(2,1)S(1)} %get-tuple-element.14), channel_id=1, source_target_pairs={{0,4},{1,45},{2,69},{3,110},{4,134},{5,175},{6,199},{16,20},{17,61... | collective-permute-start | bytes 196616 | tf_op jit(solution)/shard_map/ppermute | solution.py:186
  48.9 7.0 %collective-permute-start.2 = (bf16[128,256]{1,0:T(8,128)(2,1)S(1)}, bf16[128,256]{1,0:T(8,128)(2,1)S(1)}, u32[]{:S(2)}, u32[]{:S(2)}) collective-permute-start(bf16[128,256]{1,0:T(8,128)(2,1)S(1)} %shard_map.49.own_ref), channel_id=1, source_target_pairs={{0,16},{1,17},{2,18},{3,19},{4,20},{5,21},{6,22},{7,23},{8,24},{9,... | collective-permute-start | bytes 196616 | tf_op jit(solution)/shard_map/ppermute | solution.py:179

commit v4 on v3

--- a/solution.py
+++ b/solution.py
@@ -8,7 +8,7 @@
 from jax.sharding import Mesh, PartitionSpec as P
 
 F32, BF16 = jnp.float32, jnp.bfloat16
-AXES = ("y", "xh", "core", "mp")
+AXES = ("yk", "yp", "xh", "core", "mp")
 VMEM = pl.BlockSpec(memory_space=pltpu.VMEM)
 SMEM = pl.BlockSpec(memory_space=pltpu.SMEM)
 
@@ -35,17 +35,17 @@
     def move(y, x, c, m):
         to_y, to_x = m // x_n, m % x_n
         low = (m // z_n) ^ x ^ to_x
-        return to_y, to_x, c, low * z_n + (m % z_n + y - to_y + z_n // 2) % z_n
+        return to_y, to_x, c, low * z_n + (m % z_n + 3 * (y - to_y) + c * (z_n // 2)) % z_n
 
     whole = pairs(shape, move)
-    down = [(a, b) for a, b in whole if b % z_n <= a % z_n]
+    down = [(a, b) for a, b in whole if b % z_n < a % z_n]
     return down, [pair for pair in whole if pair not in down]
 
 
 def partial_kernel(
-    core_ref, grads_hbm, left_hbm, right_hbm, act_hbm, send_ref, keep_ref, half_ref, grads, left, act, turned, sems
+    core_ref, grads_hbm, left_hbm, right_hbm, act_hbm, send_hbm, keep_ref, half_ref, grads, left, act, turned, send, sems, send_sems
 ):
-    _, half, width = send_ref.shape
+    _, half, width = send.shape
     tiles, _, columns = act.shape
     copies = [
         pltpu.make_async_copy(grads_hbm, grads, sems.at[0]),
@@ -75,9 +75,14 @@
         for part in range(columns // width):
             piece = tile * (columns // width) + part
             block = product[:, part * width : (part + 1) * width]
-            send_ref[piece] = block[:half].astype(BF16)
+            send[piece] = block[:half].astype(BF16)
             keep_ref[piece] = block[half:]
-    copies[-1].wait()
+        part = pl.ds(tile * (columns // width), columns // width)
+        out = pltpu.make_async_copy(send.at[part], send_hbm.at[part], send_sems.at[tile])
+        out.start()
+        copies.append(out)
+    for copy in copies[2 + tiles :]:
+        copy.wait()
 
 
 def partials(shape, core, activations, out_grads, input_inverse, output_inverse, tiles=4):
@@ -87,35 +92,72 @@
     half = (input_inverse.shape[0], input_inverse.shape[1] // c_n)
     blocks = (y_n * x_n, rows // c_n, features // (y_n * x_n))
     hbm = pl.BlockSpec(memory_space=pl.ANY)
+    operands = out_grads, output_inverse, input_inverse, activations
+    operands = [pltpu.with_memory_space_constraint(a, pltpu.HBM) for a in operands]
     return pl.pallas_call(
         partial_kernel,
-        out_shape=(pltpu.VMEM(blocks, BF16), pltpu.VMEM(blocks, F32), pltpu.VMEM(half, BF16)),
+        out_shape=(pltpu.HBM(blocks, BF16), pltpu.VMEM(blocks, F32), pltpu.VMEM(half, BF16)),
         in_specs=[SMEM, hbm, hbm, hbm, hbm],
-        out_specs=(VMEM, VMEM, VMEM),
+        out_specs=(hbm, VMEM, VMEM),
         scratch_shapes=[
             pltpu.VMEM(out_grads.shape, BF16),
             pltpu.VMEM(output_inverse.shape, BF16),
             pltpu.VMEM((tiles, tokens, features // tiles), BF16),
             pltpu.VMEM((rows, tokens), BF16),
+            pltpu.VMEM(blocks, BF16),
             pltpu.SemaphoreType.DMA((3 + tiles,)),
+            pltpu.SemaphoreType.DMA((tiles,)),
         ],
-        compiler_params=pltpu.CompilerParams(vmem_limit_bytes=54 * 2**20),
-    )(core.reshape(1), out_grads, output_inverse, input_inverse, activations)
-
-
-def add_kernel(keep_ref, got_ref, total_ref):
-    for piece in range(keep_ref.shape[0]):
-        total_ref[piece] = (keep_ref[piece] + got_ref[piece].astype(F32)).astype(BF16)
-
-
-def add(keep, got):
-    return pl.pallas_call(
-        add_kernel,
-        out_shape=jax.ShapeDtypeStruct(got.shape, BF16),
+        compiler_params=pltpu.CompilerParams(vmem_limit_bytes=16 * 2**20),
+    )(core.reshape(1), *operands)
+
+
+def pieces_of(parity, count):
+    return [4 * (block // 2) + 2 * parity + block % 2 for block in range(count)]
+
+
+def first_kernel(parity_ref, keep_ref, got_ref, send_ref, rest_ref):
+    parity = parity_ref[0]
+    count = send_ref.shape[0]
+    for block, piece in enumerate(pieces_of(1 - parity, count)):
+        send_ref[block] = (keep_ref[piece] + got_ref[piece].astype(F32)).astype(BF16)
+    for block, piece in enumerate(pieces_of(parity, count)):
+        rest_ref[block] = keep_ref[piece] + got_ref[piece].astype(F32)
+
+
+def first_sum(parity, keep, got):
+    count, half, width = got.shape
+    shape = (count // 2, half, width)
+    return pl.pallas_call(
+        first_kernel,
+        out_shape=(pltpu.VMEM(shape, BF16), pltpu.VMEM(shape, F32)),
+        in_specs=[SMEM, VMEM, VMEM],
+        out_specs=(VMEM, VMEM),
+        compiler_params=pltpu.CompilerParams(vmem_limit_bytes=8 * 2**20),
+    )(parity.reshape(1), keep, got)
+
+
+def second_kernel(rest_ref, got_ref, total_hbm, total_ref, sems):
+    copies = []
+    for block in range(rest_ref.shape[0]):
+        total_ref[block] = (rest_ref[block] + got_ref[block].astype(F32)).astype(BF16)
+        if block % 2:
+            pair = pl.ds(block - 1, 2)
+            copies.append(pltpu.make_async_copy(total_ref.at[pair], total_hbm.at[pair], sems.at[block // 2]))
+            copies[-1].start()
+    for copy in copies:
+        copy.wait()
+
+
+def second_sum(rest, got):
+    return pl.pallas_call(
+        second_kernel,
+        out_shape=pltpu.HBM(got.shape, BF16),
         in_specs=[VMEM, VMEM],
-        out_specs=VMEM,
-        compiler_params=pltpu.CompilerParams(vmem_limit_bytes=16 * 2**20),
-    )(keep, got)
+        out_specs=pl.BlockSpec(memory_space=pl.ANY),
+        scratch_shapes=[pltpu.VMEM(got.shape, BF16), pltpu.SemaphoreType.DMA((got.shape[0] // 2,))],
+        compiler_params=pltpu.CompilerParams(vmem_limit_bytes=8 * 2**20),
+    )(rest, got)
 
 
 def sum_kernel(pieces_ref, _, total_ref):
@@ -125,14 +167,14 @@
     total_ref[...] = total.astype(BF16)
 
 
-def sum_pieces(pieces, first):
+def sum_pieces(pieces, held):
     return pl.pallas_call(
         sum_kernel,
         out_shape=jax.ShapeDtypeStruct(pieces.shape[1:], BF16),
         in_specs=[VMEM, VMEM],
         out_specs=VMEM,
         compiler_params=pltpu.CompilerParams(vmem_limit_bytes=8 * 2**20),
-    )(pieces, first)
+    )(pieces, held)
 
 
 def right_kernel(core_ref, own_ref, other_ref, near_ref, far_ref, out_ref):
@@ -173,18 +215,27 @@
 
 
 def per_device(shape, activations, out_grads, input_inverse, output_inverse):
-    core = lax.axis_index("core")
+    core, parity = lax.axis_index("core"), lax.axis_index("yp")
+    y_n = shape[0]
 
     def to_core(a):
         return lax.ppermute(a, AXES, pairs(shape, lambda y, x, c, m: (y, x, 1 - c, m)))
 
+    def to_y(a):
+        def move(y, x, c, m):
+            return (((y + c) % y_n ^ 1) - c) % y_n, x, c, m
+
+        return lax.ppermute(a, AXES, pairs(shape, move))
+
     send, keep, half = partials(shape, core, activations, out_grads, input_inverse, output_inverse)
-    down, up = spread(shape)
-    near = lax.ppermute(half, AXES, down)
-    total = add(keep, to_core(send))
+    lower, higher = spread(shape)
+    near = lax.ppermute(half, AXES, lower)
+    got = to_core(send)
+    send, rest = first_sum(parity, keep, got)
+    total = second_sum(rest, to_y(send))
     total, half = lax.optimization_barrier((total, half))
-    far = lax.ppermute(half, AXES, up)
-    pieces = lax.all_to_all(total, ("y", "xh"), 0, 0)
+    far = lax.ppermute(half, AXES, higher)
+    pieces = lax.all_to_all(total, ("yk", "xh"), 0, 0)
     near = hold(near)
     gathered = sum_pieces(pieces, near)
     return right(core, gathered, to_core(gathered), near, far)
@@ -193,8 +244,8 @@
 def solution(mesh):
     dp_count, mp_count = mesh.devices.shape
     shape = (dp_count // 4, 2, 2, mp_count)
-    split = Mesh(mesh.devices.reshape(shape), AXES)
-    dp = AXES[:3]
+    split = Mesh(mesh.devices.reshape(shape[0] // 2, 2, *shape[1:]), AXES)
+    dp = AXES[:4]
     in_specs = (P(dp, None), P(dp, "mp"), P("mp", None), P("mp", None))
     return jax.shard_map(
         functools.partial(per_device, shape),

time: 57 us -> 54.3 us (0.953)
  the two profiles are of different devices: /device:TPU:1 before, /device:TPU:315 now
where the time goes in v4:
time: 54.3 us; the launch traced here: 54 us
  starting transfers between devices  30.5 us (56%)
  waiting for transfers between devices  17.6 us (32%)
  Pallas kernels  5.82 us (11%)
    ppermute x2, starting transfers between devices, to_core(): lax.ppermute(a, AXES, pairs(shape, lambda y, x, c, m: (y, x, 1 - c, m)))  18.3 us
    ppermute x1, waiting for transfers between devices, to_y(): return lax.ppermute(a, AXES, pairs(shape, move))  7.48 us
    all_to_all x1, waiting for transfers between devices, per_device(): pieces = lax.all_to_all(total, ('yk', 'xh'), 0, 0)  6.79 us
    all_to_all x1, starting transfers between devices, per_device(): pieces = lax.all_to_all(total, ('yk', 'xh'), 0, 0)  6.42 us
    pallas_call x1, Pallas kernels, partials(): pl.pallas_call(partial_kernel, out_shape=(pltpu.HBM(blocks, BF16), pltpu....  3.9 us
    ppermute x2, waiting for transfers between devices, to_core(): lax.ppermute(a, AXES, pairs(shape, lambda y, x, c, m: (y, x, 1 - c, m)))  3.34 us
    ppermute x1, starting transfers between devices, per_device(): near = lax.ppermute(half, AXES, lower)  3.12 us
    ppermute x1, starting transfers between devices, to_y(): return lax.ppermute(a, AXES, pairs(shape, move))  1.92 us
  transfers between devices with their start and end apart: 6, of which 4 were waited for; matrix products, arithmetic and copies ran while one was open for 0% of the time, Pallas kernels for 2%

profile of v4, /device:TPU:315, one launch (start us, length us, event | category | flops | bytes accessed | tf_op | source)
XLA Modules:
  0.0 54.0 jit_solution(2745580052327031034)
XLA Ops:
  0.0 3.9 %shard_map.46 = (bf16[16,128,256]{2,1,0:T(8,128)(2,1)}, f32[16,128,256]{2,1,0:T(8,128)S(1)}, bf16[256,128]{1,0:T(8,128)(2,1)S(1)}) custom-call(s32[1]{0:T(128)} %bitcast.core_ref, bf16[512,256]{1,0:T(8,128)(2,1)} %grads_hbm.1, bf16[256,256]{1,0:T(8,128)(2,1)} %left_hbm.1, bf16[256,256]{1,0:T(8,128)(2,1)} %right_hbm.1, bf16[512,4096]{1,0:T(8,128)(2,1)} %act_hbm.1), custom_call_target="tpu_custom_call" | custom-call | tf_op jit(solution)/shard_map/pallas_call | solution.py:97
  3.9 2.6 %collective-permute-start = (bf16[16,128,256]{2,1,0:T(8,128)(2,1)}, bf16[16,128,256]{2,1,0:T(8,128)(2,1)S(1)}, u32[]{:S(2)}, u32[]{:S(2)}) collective-permute-start(bf16[16,128,256]{2,1,0:T(8,128)(2,1)} %get-tuple-element.13), channel_id=1, source_target_pairs={{0,16},{1,17},{2,18},{3,19},{4,20},{5,21},{6,22},{7,23},{8,24},{9,... | collective-permute-start | bytes 3145736 | tf_op jit(solution)/shard_map/ppermute | solution.py:222
  6.5 2.5 %collective-permute-done.got_ref = bf16[16,128,256]{2,1,0:T(8,128)(2,1)S(1)} collective-permute-done((bf16[16,128,256]{2,1,0:T(8,128)(2,1)}, bf16[16,128,256]{2,1,0:T(8,128)(2,1)S(1)}, u32[]{:S(2)}, u32[]{:S(2)}) %collective-permute-start) | collective-permute-done | bytes 1048608 | tf_op jit(solution)/shard_map/ppermute | solution.py:222
  9.0 0.2 shard_map.47
  9.2 1.9 %collective-permute-start.1 = (bf16[8,128,256]{2,1,0:T(8,128)(2,1)S(1)}, bf16[8,128,256]{2,1,0:T(8,128)(2,1)S(1)}, u32[]{:S(2)}, u32[]{:S(2)}) collective-permute-start(bf16[8,128,256]{2,1,0:T(8,128)(2,1)S(1)} %get-tuple-element.15), channel_id=1, source_target_pairs={{0,64},{1,65},{2,66},{3,67},{4,68},{5,69},{6,70},{7,71},{8,72},{9,... | collective-permute-start | bytes 1572872 | tf_op jit(solution)/shard_map/ppermute | solution.py:228
  11.1 3.1 %collective-permute-start.2 = (bf16[256,128]{1,0:T(8,128)(2,1)S(1)}, bf16[256,128]{1,0:T(8,128)(2,1)S(1)}, u32[]{:S(2)}, u32[]{:S(2)}) collective-permute-start(bf16[256,128]{1,0:T(8,128)(2,1)S(1)} %get-tuple-element.18), channel_id=1, source_target_pairs={{3,104},{6,197},{7,238},{12,394},{13,419},{14,457},{15,482},{20,14... | collective-permute-start | bytes 196616 | tf_op jit(solution)/shard_map/ppermute | solution.py:232
  14.2 7.5 %collective-permute-done.1.got_ref = bf16[8,128,256]{2,1,0:T(8,128)(2,1)S(1)} collective-permute-done((bf16[8,128,256]{2,1,0:T(8,128)(2,1)S(1)}, bf16[8,128,256]{2,1,0:T(8,128)(2,1)S(1)}, u32[]{:S(2)}, u32[]{:S(2)}) %collective-permute-start.1) | collective-permute-done | bytes 524320 | tf_op jit(solution)/shard_map/ppermute | solution.py:228
  21.7 0.9 %shard_map.48 = bf16[8,128,256]{2,1,0:T(8,128)(2,1)} custom-call(f32[8,128,256]{2,1,0:T(8,128)S(1)} %get-tuple-element.14.rest_ref, bf16[8,128,256]{2,1,0:T(8,128)(2,1)S(1)} %collective-permute-done.1.got_ref), custom_call_target="tpu_custom_call" | custom-call | tf_op jit(solution)/shard_map/pallas_call | solution.py:153
  22.6 6.4 %all-to-all-start = ((bf16[8,128,256]{2,1,0:T(8,128)(2,1)}), bf16[8,128,256]{2,1,0:T(8,128)(2,1)S(1)}, u32[]{:S(2)}, u32[]{:S(2)}) async-start(bf16[8,128,256]{2,1,0:T(8,128)(2,1)} %shard_map.48), calls=%async_computation | async-start | bytes 1048576 | tf_op jit(solution)/shard_map/all_to_all | solution.py:238
  29.0 0.0 collective-permute-done.2.block_ref
  29.0 0.7 %collective-permute-start.4 = (bf16[256,128]{1,0:T(8,128)(2,1)S(1)}, bf16[256,128]{1,0:T(8,128)(2,1)S(1)}, u32[]{:S(2)}, u32[]{:S(2)}) collective-permute-start(bf16[256,128]{1,0:T(8,128)(2,1)S(1)} %get-tuple-element.18), channel_id=1, source_target_pairs={{0,0},{1,41},{2,71},{4,134},{5,175},{8,268},{9,293},{10,331},{11,3... | collective-permute-start | bytes 196616 | tf_op jit(solution)/shard_map/ppermute | solution.py:237
  29.7 6.8 %all-to-all-done.pieces_ref = bf16[8,128,256]{2,1,0:T(8,128)(2,1)S(1)} async-done(((bf16[8,128,256]{2,1,0:T(8,128)(2,1)}), bf16[8,128,256]{2,1,0:T(8,128)(2,1)S(1)}, u32[]{:S(2)}, u32[]{:S(2)}) %all-to-all-start) | async-done | bytes 524320 | tf_op jit(solution)/shard_map/all_to_all | solution.py:238
  36.5 0.1 shard_map.50.own_ref
  36.5 15.8 %collective-permute-start.3 = (bf16[128,256]{1,0:T(8,128)(2,1)S(1)}, bf16[128,256]{1,0:T(8,128)(2,1)S(1)}, u32[]{:S(2)}, u32[]{:S(2)}) collective-permute-start(bf16[128,256]{1,0:T(8,128)(2,1)S(1)} %shard_map.50.own_ref), channel_id=1, source_target_pairs={{0,16},{1,17},{2,18},{3,19},{4,20},{5,21},{6,22},{7,23},{8,24},{9,... | collective-permute-start | bytes 196616 | tf_op jit(solution)/shard_map/ppermute | solution.py:222
  52.3 0.0 collective-permute-done.4.far_ref
  52.3 0.9 %collective-permute-done.3.other_ref = bf16[128,256]{1,0:T(8,128)(2,1)S(1)} collective-permute-done((bf16[128,256]{1,0:T(8,128)(2,1)S(1)}, bf16[128,256]{1,0:T(8,128)(2,1)S(1)}, u32[]{:S(2)}, u32[]{:S(2)}) %collective-permute-start.3) | collective-permute-done | bytes 65568 | tf_op jit(solution)/shard_map/ppermute | solution.py:222
  53.2 0.8 %shard_map.51 = bf16[256,128]{1,0:T(8,128)(2,1)} custom-call(s32[1]{0:T(128)} %bitcast.core_ref, bf16[128,256]{1,0:T(8,128)(2,1)S(1)} %shard_map.50.own_ref, bf16[128,256]{1,0:T(8,128)(2,1)S(1)} %collective-permute-done.3.other_ref, bf16[256,128]{1,0:T(8,128)(2,1)S(1)} %shard_map.49._.near_ref, bf16[256,128]{1,0:T(8,128)(2,1)S(1)} %collective-permute-done.4.far_ref), custom_call_target="tpu_custom_call" | custom-call | tf_op jit(solution)/shard_map/pallas_call | solution.py:193
  (1 shorter events, 0.0 us)
Async XLA Ops:
  3.9 5.1 %collective-permute-start = (bf16[16,128,256]{2,1,0:T(8,128)(2,1)}, bf16[16,128,256]{2,1,0:T(8,128)(2,1)S(1)}, u32[]{:S(2)}, u32[]{:S(2)}) collective-permute-start(bf16[16,128,256]{2,1,0:T(8,128)(2,1)} %get-tuple-element.13), channel_id=1, source_target_pairs={{0,16},{1,17},{2,18},{3,19},{4,20},{5,21},{6,22},{7,23},{8,24},{9,... | collective-permute-start | bytes 3145736 | tf_op jit(solution)/shard_map/ppermute | solution.py:222
  9.2 12.5 %collective-permute-start.1 = (bf16[8,128,256]{2,1,0:T(8,128)(2,1)S(1)}, bf16[8,128,256]{2,1,0:T(8,128)(2,1)S(1)}, u32[]{:S(2)}, u32[]{:S(2)}) collective-permute-start(bf16[8,128,256]{2,1,0:T(8,128)(2,1)S(1)} %get-tuple-element.15), channel_id=1, source_target_pairs={{0,64},{1,65},{2,66},{3,67},{4,68},{5,69},{6,70},{7,71},{8,72},{9,... | collective-permute-start | bytes 1572872 | tf_op jit(solution)/shard_map/ppermute | solution.py:228
  11.1 17.9 %collective-permute-start.2 = (bf16[256,128]{1,0:T(8,128)(2,1)S(1)}, bf16[256,128]{1,0:T(8,128)(2,1)S(1)}, u32[]{:S(2)}, u32[]{:S(2)}) collective-permute-start(bf16[256,128]{1,0:T(8,128)(2,1)S(1)} %get-tuple-element.18), channel_id=1, source_target_pairs={{3,104},{6,197},{7,238},{12,394},{13,419},{14,457},{15,482},{20,14... | collective-permute-start | bytes 196616 | tf_op jit(solution)/shard_map/ppermute | solution.py:232
  22.6 13.9 %all-to-all-start = ((bf16[8,128,256]{2,1,0:T(8,128)(2,1)}), bf16[8,128,256]{2,1,0:T(8,128)(2,1)S(1)}, u32[]{:S(2)}, u32[]{:S(2)}) async-start(bf16[8,128,256]{2,1,0:T(8,128)(2,1)} %shard_map.48), calls=%async_computation | async-start | bytes 1048576 | tf_op jit(solution)/shard_map/all_to_all | solution.py:238
  29.0 23.3 %collective-permute-start.4 = (bf16[256,128]{1,0:T(8,128)(2,1)S(1)}, bf16[256,128]{1,0:T(8,128)(2,1)S(1)}, u32[]{:S(2)}, u32[]{:S(2)}) collective-permute-start(bf16[256,128]{1,0:T(8,128)(2,1)S(1)} %get-tuple-element.18), channel_id=1, source_target_pairs={{0,0},{1,41},{2,71},{4,134},{5,175},{8,268},{9,293},{10,331},{11,3... | collective-permute-start | bytes 196616 | tf_op jit(solution)/shard_map/ppermute | solution.py:237
  36.5 16.6 %collective-permute-start.3 = (bf16[128,256]{1,0:T(8,128)(2,1)S(1)}, bf16[128,256]{1,0:T(8,128)(2,1)S(1)}, u32[]{:S(2)}, u32[]{:S(2)}) collective-permute-start(bf16[128,256]{1,0:T(8,128)(2,1)S(1)} %shard_map.50.own_ref), channel_id=1, source_target_pairs={{0,16},{1,17},{2,18},{3,19},{4,20},{5,21},{6,22},{7,23},{8,24},{9,... | collective-permute-start | bytes 196616 | tf_op jit(solution)/shard_map/ppermute | solution.py:222

commit v5 on v4

v5 whole, which is shorter than its diff:
```python
import functools

import jax
import jax.numpy as jnp
from jax import lax
from jax.experimental import pallas as pl
from jax.experimental.pallas import tpu as pltpu
from jax.sharding import Mesh, PartitionSpec as P

F32, BF16 = jnp.float32, jnp.bfloat16
AXES = ("yk", "yp", "xh", "core", "mp")
VMEM = pl.BlockSpec(memory_space=pltpu.VMEM)
SMEM = pl.BlockSpec(memory_space=pltpu.SMEM)


def pairs(shape, move):
    y_n, x_n, c_n, m_n = shape

    def flat(y, x, c, m):
        return ((y * x_n + x) * c_n + c) * m_n + m

    return [
        (flat(y, x, c, m), flat(*move(y, x, c, m)))
        for y in range(y_n)
        for x in range(x_n)
        for c in range(c_n)
        for m in range(m_n)
    ]


def spread(shape):
    y_n, x_n, _, m_n = shape
    z_n = m_n // 2

    def move(y, x, c, m):
        to_y, to_x = m // x_n, m % x_n
        low = (m // z_n) ^ x ^ to_x
        return to_y, to_x, c, low * z_n + (m % z_n + 3 * (y - to_y) + c * (z_n // 2)) % z_n

    whole = pairs(shape, move)
    down = [(a, b) for a, b in whole if b % z_n < a % z_n]
    return down, [pair for pair in whole if pair not in down]


def products(parity, act_hbm, act, turned, send_ref, keep_ref, sems):
    tiles, _, columns = act.shape
    half, width = send_ref.shape[1:]
    copies = []
    for tile in range(tiles):
        first = pl.multiple_of((2 * tile + parity) * columns, columns)
        copies.append(pltpu.make_async_copy(act_hbm.at[:, pl.ds(first, columns)], act.at[tile], sems.at[tile]))
        copies[-1].start()

    def run():
        for tile in range(tiles):
            copies[tile].wait()
            product = jnp.dot(turned[...], act[tile], preferred_element_type=F32)
            for part in range(columns // width):
                piece = tile * (columns // width) + part
                block = product[:, part * width : (part + 1) * width]
                send_ref[piece] = block[:half].astype(BF16)
                keep_ref[piece] = block[half:]

    return run


def leading_kernel(
    at_ref, grads_hbm, left_hbm, right_hbm, act_hbm, send_ref, keep_ref, turned, half_ref, grads, left, act, sems, own
):
    core, parity = at_ref[0], at_ref[1]
    half = send_ref.shape[1]
    copies = [
        pltpu.make_async_copy(grads_hbm, grads, own.at[0]),
        pltpu.make_async_copy(left_hbm, left, own.at[1]),
    ]
    for copy in copies:
        copy.start()
    run = products(1 - parity, act_hbm, act, turned, send_ref, keep_ref, sems)
    narrow = half_ref.shape[1]
    source = right_hbm.at[:, pl.ds(pl.multiple_of(core * narrow, narrow), narrow)]
    last = pltpu.make_async_copy(source, half_ref, own.at[2])
    last.start()
    for copy in copies:
        copy.wait()
    for part in range(2):
        first = pl.multiple_of((core ^ (1 - part)) * half, half)
        turned[part * half : (part + 1) * half] = lax.dot_general(
            left[pl.ds(first, half)],
            grads[...],
            (((1,), (1,)), ((), ())),
            preferred_element_type=F32,
        ).astype(BF16)
    run()
    last.wait()


def trailing_kernel(at_ref, turned, act_hbm, send_ref, keep_ref, act, sems):
    products(at_ref[1], act_hbm, act, turned, send_ref, keep_ref, sems)()


def sizes(shape, activations, out_grads):
    y_n, x_n, c_n, _ = shape
    tokens, features = activations.shape
    rows = out_grads.shape[1]
    tiles = y_n // 2
    blocks = (tiles * x_n, rows // c_n, features // (y_n * x_n))
    cost = pl.CostEstimate(
        flops=rows * tokens * features, bytes_accessed=tokens * features, transcendentals=0
    )
    return blocks, (tiles, tokens, features // y_n), cost


def leading(shape, at, activations, out_grads, input_inverse, output_inverse):
    blocks, tiles, cost = sizes(shape, activations, out_grads)
    hbm = pl.BlockSpec(memory_space=pl.ANY)
    operands = out_grads, output_inverse, input_inverse, activations
    operands = [pltpu.with_memory_space_constraint(a, pltpu.HBM) for a in operands]
    half = (input_inverse.shape[0], input_inverse.shape[1] // 2)
    return pl.pallas_call(
        leading_kernel,
        out_shape=(
            pltpu.VMEM(blocks, BF16),
            pltpu.VMEM(blocks, F32),
            pltpu.VMEM(out_grads.shape[::-1], BF16),
            pltpu.VMEM(half, BF16),
        ),
        in_specs=[SMEM, hbm, hbm, hbm, hbm],
        out_specs=(VMEM, VMEM, VMEM, VMEM),
        scratch_shapes=[
            pltpu.VMEM(out_grads.shape, BF16),
            pltpu.VMEM(output_inverse.shape, BF16),
            pltpu.VMEM(tiles, BF16),
            pltpu.SemaphoreType.DMA((tiles[0],)),
            pltpu.SemaphoreType.DMA((3,)),
        ],
        compiler_params=pltpu.CompilerParams(vmem_limit_bytes=12 * 2**20),
        cost_estimate=cost,
    )(at, *operands)


def trailing(shape, at, activations, out_grads, turned):
    blocks, tiles, cost = sizes(shape, activations, out_grads)
    return pl.pallas_call(
        trailing_kernel,
        out_shape=(pltpu.VMEM(blocks, BF16), pltpu.VMEM(blocks, F32)),
        in_specs=[SMEM, VMEM, pl.BlockSpec(memory_space=pl.ANY)],
        out_specs=(VMEM, VMEM),
        scratch_shapes=[
            pltpu.VMEM(tiles, BF16),
            pltpu.SemaphoreType.DMA((tiles[0],)),
        ],
        compiler_params=pltpu.CompilerParams(vmem_limit_bytes=12 * 2**20),
        cost_estimate=cost,
    )(at, turned, pltpu.with_memory_space_constraint(activations, pltpu.HBM))


def first_kernel(keep_ref, got_ref, send_ref):
    for block in range(send_ref.shape[0]):
        send_ref[block] = (keep_ref[block] + got_ref[block].astype(F32)).astype(BF16)


def first_sum(keep, got):
    return pl.pallas_call(
        first_kernel,
        out_shape=pltpu.VMEM(got.shape, BF16),
        in_specs=[VMEM, VMEM],
        out_specs=VMEM,
        compiler_params=pltpu.CompilerParams(vmem_limit_bytes=8 * 2**20),
    )(keep, got)


def second_kernel(keep_ref, more_ref, got_ref, total_hbm, total_ref, sems):
    copies = []
    for block in range(keep_ref.shape[0]):
        total = keep_ref[block] + got_ref[block].astype(F32) + more_ref[block].astype(F32)
        total_ref[block] = total.astype(BF16)
        if block % 2:
            pair = pl.ds(block - 1, 2)
            copies.append(pltpu.make_async_copy(total_ref.at[pair], total_hbm.at[pair], sems.at[block // 2]))
            copies[-1].start()
    for copy in copies:
        copy.wait()


def second_sum(keep, more, got):
    return pl.pallas_call(
        second_kernel,
        out_shape=pltpu.HBM(got.shape, BF16),
        in_specs=[VMEM, VMEM, VMEM],
        out_specs=pl.BlockSpec(memory_space=pl.ANY),
        scratch_shapes=[pltpu.VMEM(got.shape, BF16), pltpu.SemaphoreType.DMA((got.shape[0] // 2,))],
        compiler_params=pltpu.CompilerParams(vmem_limit_bytes=8 * 2**20),
    )(keep, more, got)


def sum_kernel(pieces_ref, _, total_ref):
    total = pieces_ref[0].astype(F32)
    for piece in range(1, pieces_ref.shape[0]):
        total += pieces_ref[piece].astype(F32)
    total_ref[...] = total.astype(BF16)


def sum_pieces(pieces, held):
    return pl.pallas_call(
        sum_kernel,
        out_shape=jax.ShapeDtypeStruct(pieces.shape[1:], BF16),
        in_specs=[VMEM, VMEM],
        out_specs=VMEM,
        compiler_params=pltpu.CompilerParams(vmem_limit_bytes=8 * 2**20),
    )(pieces, held)


def right_kernel(core_ref, own_ref, other_ref, near_ref, far_ref, out_ref):
    half = own_ref.shape[0]
    core = core_ref[0]
    block = near_ref[...] + far_ref[...]
    for ref, index in ((own_ref, core), (other_ref, 1 - core)):
        first = pl.multiple_of(index * half, half)
        out_ref[pl.ds(first, half)] = jnp.dot(
            ref[...], block, preferred_element_type=F32
        ).astype(BF16)


def right(core, own, other, near, far):
    half, width = own.shape
    return pl.pallas_call(
        right_kernel,
        out_shape=jax.ShapeDtypeStruct((2 * half, width // 2), BF16),
        in_specs=[SMEM, VMEM, VMEM, VMEM, VMEM],
        out_specs=VMEM,
        compiler_params=pltpu.CompilerParams(vmem_limit_bytes=8 * 2**20),
    )(core.reshape(1), own, other, near, far)


def hold_kernel(block_ref, out_ref):
    out_ref[...] = block_ref[...]


def hold(block):
    return pl.pallas_call(
        hold_kernel,
        out_shape=jax.ShapeDtypeStruct(block.shape, BF16),
        in_specs=[VMEM],
        out_specs=VMEM,
        compiler_params=pltpu.CompilerParams(vmem_limit_bytes=4 * 2**20),
        cost_estimate=pl.CostEstimate(flops=5 * 10**10, bytes_accessed=2**17, transcendentals=0),
    )(block)


def per_device(shape, activations, out_grads, input_inverse, output_inverse):
    core, parity = lax.axis_index("core"), lax.axis_index("yp")
    y_n = shape[0]

    def to_core(a):
        return lax.ppermute(a, AXES, pairs(shape, lambda y, x, c, m: (y, x, 1 - c, m)))

    def to_y(a):
        def move(y, x, c, m):
            return (((y + c) % y_n ^ 1) - c) % y_n, x, c, m

        return lax.ppermute(a, AXES, pairs(shape, move))

    at = jnp.stack([core, parity])
    send, keep, turned, half = leading(shape, at, activations, out_grads, input_inverse, output_inverse)
    lower, higher = spread(shape)
    near = lax.ppermute(half, AXES, lower)
    got = to_core(send)
    send, rest = trailing(shape, at, activations, out_grads, turned)
    send_y, send = lax.optimization_barrier((first_sum(keep, got), send))
    got_y = to_y(send_y)
    total = second_sum(rest, got_y, to_core(send))
    total, half = lax.optimization_barrier((total, half))
    far = lax.ppermute(half, AXES, higher)
    pieces = lax.all_to_all(total, ("yk", "xh"), 0, 0)
    near = hold(near)
    gathered = sum_pieces(pieces, near)
    return right(core, gathered, to_core(gathered), near, far)


def solution(mesh):
    dp_count, mp_count = mesh.devices.shape
    shape = (dp_count // 4, 2, 2, mp_count)
    split = Mesh(mesh.devices.reshape(shape[0] // 2, 2, *shape[1:]), AXES)
    dp = AXES[:4]
    in_specs = (P(dp, None), P(dp, "mp"), P("mp", None), P("mp", None))
    return jax.shard_map(
        functools.partial(per_device, shape),
        mesh=split,
        in_specs=in_specs,
        out_specs=P("mp", dp),
        check_vma=False,
    )
```

time: 54.3 us -> 53.3 us (0.982)
  the two profiles are of different devices: /device:TPU:315 before, /device:TPU:1 now
where the time goes in v5:
time: 53.3 us; the launch traced here: 53 us
  starting transfers between devices  30.5 us (57%)
  waiting for transfers between devices  14.1 us (26%)
  Pallas kernels  8.11 us (15%)
    ppermute x3, starting transfers between devices, to_core(): lax.ppermute(a, AXES, pairs(shape, lambda y, x, c, m: (y, x, 1 - c, m)))  13.4 us
    ppermute x1, starting transfers between devices, per_device(): far = lax.ppermute(half, AXES, higher)  10.6 us
    all_to_all x1, waiting for transfers between devices, per_device(): pieces = lax.all_to_all(total, ('yk', 'xh'), 0, 0)  6.63 us
    ppermute x1, waiting for transfers between devices, to_y(): return lax.ppermute(a, AXES, pairs(shape, move))  6.6 us
    all_to_all x1, starting transfers between devices, per_device(): pieces = lax.all_to_all(total, ('yk', 'xh'), 0, 0)  3.92 us
    pallas_call x1, Pallas kernels, leading(): pl.pallas_call(leading_kernel, out_shape=(pltpu.VMEM(blocks, BF16), pltpu...  3.43 us
    pallas_call x1, Pallas kernels, trailing(): pl.pallas_call(trailing_kernel, out_shape=(pltpu.VMEM(blocks, BF16), pltp...  2.83 us
    ppermute x1, starting transfers between devices, to_y(): return lax.ppermute(a, AXES, pairs(shape, move))  1.92 us
  transfers between devices with their start and end apart: 7, of which 3 were waited for; matrix products, arithmetic and copies ran while one was open for 0% of the time, Pallas kernels for 7%

profile of v5, /device:TPU:1, one launch (start us, length us, event | category | flops | bytes accessed | tf_op | source)
XLA Modules:
  0.0 53.0 jit_solution(603741772727102783)
XLA Ops:
  0.0 0.1 pad_add_fusion.at_ref
  0.1 3.4 %shard_map.46 = (bf16[8,128,256]{2,1,0:T(8,128)(2,1)S(1)}, f32[8,128,256]{2,1,0:T(8,128)S(1)}, bf16[256,512]{1,0:T(8,128)(2,1)S(1)}, bf16[256,128]{1,0:T(8,128)(2,1)S(1)}) custom-call(s32[2]{0:T(128)S(1)} %pad_add_fusion.at_ref, bf16[512,256]{1,0:T(8,128)(2,1)} %grads_hbm.1, bf16[256,256]{1,0:T(8,128)(2,1)} %left_hbm.1, bf16[256,256]{1,0:T(8,128)(2,1)} %right_hbm.1, ...), custom_call_target="tpu_custom_call" | custom-call | flops 536870912 | bytes 2097152 | tf_op jit(solution)/shard_map/pallas_call | solution.py:119
  3.5 8.8 %collective-permute-start = (bf16[8,128,256]{2,1,0:T(8,128)(2,1)S(1)}, bf16[8,128,256]{2,1,0:T(8,128)(2,1)S(1)}, u32[]{:S(2)}, u32[]{:S(2)}) collective-permute-start(bf16[8,128,256]{2,1,0:T(8,128)(2,1)S(1)} %get-tuple-element.18), channel_id=1, source_target_pairs={{0,16},{1,17},{2,18},{3,19},{4,20},{5,21},{6,22},{7,23},{8,24},{9,... | collective-permute-start | bytes 1572872 | tf_op jit(solution)/shard_map/ppermute | solution.py:255
  12.3 2.8 %shard_map.47 = (bf16[8,128,256]{2,1,0:T(8,128)(2,1)S(1)}, f32[8,128,256]{2,1,0:T(8,128)S(1)}) custom-call(s32[2]{0:T(128)S(1)} %pad_add_fusion.at_ref, bf16[256,512]{1,0:T(8,128)(2,1)S(1)} %get-tuple-element.15.turned, bf16[512,4096]{1,0:T(8,128)(2,1)} %act_hbm.3), custom_call_target="tpu_custom_call" | custom-call | flops 536870912 | bytes 2097152 | tf_op jit(solution)/shard_map/pallas_call | solution.py:143
  15.2 0.0 collective-permute-done.got_ref
  15.2 0.1 shard_map.48
  15.3 1.9 %collective-permute-start.1 = (bf16[8,128,256]{2,1,0:T(8,128)(2,1)S(1)}, bf16[8,128,256]{2,1,0:T(8,128)(2,1)S(1)}, u32[]{:S(2)}, u32[]{:S(2)}) collective-permute-start(bf16[8,128,256]{2,1,0:T(8,128)(2,1)S(1)} %shard_map.48), channel_id=1, source_target_pairs={{0,64},{1,65},{2,66},{3,67},{4,68},{5,69},{6,70},{7,71},{8,72},{9,... | collective-permute-start | bytes 1572872 | tf_op jit(solution)/shard_map/ppermute | solution.py:261
  17.2 1.9 %collective-permute-start.2 = (bf16[8,128,256]{2,1,0:T(8,128)(2,1)S(1)}, bf16[8,128,256]{2,1,0:T(8,128)(2,1)S(1)}, u32[]{:S(2)}, u32[]{:S(2)}) collective-permute-start(bf16[8,128,256]{2,1,0:T(8,128)(2,1)S(1)} %get-tuple-element.21), channel_id=1, source_target_pairs={{0,16},{1,17},{2,18},{3,19},{4,20},{5,21},{6,22},{7,23},{8,24},{9,... | collective-permute-start | bytes 1572872 | tf_op jit(solution)/shard_map/ppermute | solution.py:255
  19.1 0.7 %collective-permute-start.3 = (bf16[256,128]{1,0:T(8,128)(2,1)S(1)}, bf16[256,128]{1,0:T(8,128)(2,1)S(1)}, u32[]{:S(2)}, u32[]{:S(2)}) collective-permute-start(bf16[256,128]{1,0:T(8,128)(2,1)S(1)} %get-tuple-element.24), channel_id=1, source_target_pairs={{3,104},{6,197},{7,238},{12,394},{13,419},{14,457},{15,482},{20,14... | collective-permute-start | bytes 196616 | tf_op jit(solution)/shard_map/ppermute | solution.py:266
  19.8 6.6 %collective-permute-done.1.more_ref = bf16[8,128,256]{2,1,0:T(8,128)(2,1)S(1)} collective-permute-done((bf16[8,128,256]{2,1,0:T(8,128)(2,1)S(1)}, bf16[8,128,256]{2,1,0:T(8,128)(2,1)S(1)}, u32[]{:S(2)}, u32[]{:S(2)}) %collective-permute-start.1) | collective-permute-done | bytes 524320 | tf_op jit(solution)/shard_map/ppermute | solution.py:261
  26.4 0.0 collective-permute-done.2.got_ref
  26.4 0.9 %shard_map.49 = bf16[8,128,256]{2,1,0:T(8,128)(2,1)} custom-call(f32[8,128,256]{2,1,0:T(8,128)S(1)} %get-tuple-element.16.keep_ref, bf16[8,128,256]{2,1,0:T(8,128)(2,1)S(1)} %collective-permute-done.1.more_ref, bf16[8,128,256]{2,1,0:T(8,128)(2,1)S(1)} %collective-permute-done.2.got_ref), custom_call_target="tpu_custom_call" | custom-call | tf_op jit(solution)/shard_map/pallas_call | solution.py:186
  27.3 3.9 %all-to-all-start = ((bf16[8,128,256]{2,1,0:T(8,128)(2,1)}), bf16[8,128,256]{2,1,0:T(8,128)(2,1)S(1)}, u32[]{:S(2)}, u32[]{:S(2)}) async-start(bf16[8,128,256]{2,1,0:T(8,128)(2,1)} %shard_map.49), calls=%async_computation | async-start | bytes 1048576 | tf_op jit(solution)/shard_map/all_to_all | solution.py:274
  31.2 0.0 collective-permute-done.3.block_ref
  31.2 10.6 %collective-permute-start.5 = (bf16[256,128]{1,0:T(8,128)(2,1)S(1)}, bf16[256,128]{1,0:T(8,128)(2,1)S(1)}, u32[]{:S(2)}, u32[]{:S(2)}) collective-permute-start(bf16[256,128]{1,0:T(8,128)(2,1)S(1)} %get-tuple-element.24), channel_id=1, source_target_pairs={{0,0},{1,41},{2,71},{4,134},{5,175},{8,268},{9,293},{10,331},{11,3... | collective-permute-start | bytes 196616 | tf_op jit(solution)/shard_map/ppermute | solution.py:273
  41.9 6.6 %all-to-all-done.pieces_ref = bf16[8,128,256]{2,1,0:T(8,128)(2,1)S(1)} async-done(((bf16[8,128,256]{2,1,0:T(8,128)(2,1)}), bf16[8,128,256]{2,1,0:T(8,128)(2,1)S(1)}, u32[]{:S(2)}, u32[]{:S(2)}) %all-to-all-start) | async-done | bytes 524320 | tf_op jit(solution)/shard_map/all_to_all | solution.py:274
  48.5 0.1 shard_map.51.own_ref
  48.6 2.7 %collective-permute-start.4 = (bf16[128,256]{1,0:T(8,128)(2,1)S(1)}, bf16[128,256]{1,0:T(8,128)(2,1)S(1)}, u32[]{:S(2)}, u32[]{:S(2)}) collective-permute-start(bf16[128,256]{1,0:T(8,128)(2,1)S(1)} %shard_map.51.own_ref), channel_id=1, source_target_pairs={{0,16},{1,17},{2,18},{3,19},{4,20},{5,21},{6,22},{7,23},{8,24},{9,... | collective-permute-start | bytes 196616 | tf_op jit(solution)/shard_map/ppermute | solution.py:255
  51.3 0.0 collective-permute-done.5.far_ref
  51.3 0.9 %collective-permute-done.4.other_ref = bf16[128,256]{1,0:T(8,128)(2,1)S(1)} collective-permute-done((bf16[128,256]{1,0:T(8,128)(2,1)S(1)}, bf16[128,256]{1,0:T(8,128)(2,1)S(1)}, u32[]{:S(2)}, u32[]{:S(2)}) %collective-permute-start.4) | collective-permute-done | bytes 65568 | tf_op jit(solution)/shard_map/ppermute | solution.py:255
  52.2 0.8 %shard_map.52 = bf16[256,128]{1,0:T(8,128)(2,1)} custom-call(s32[1]{0:T(128)} %bitcast.core_ref, bf16[128,256]{1,0:T(8,128)(2,1)S(1)} %shard_map.51.own_ref, bf16[128,256]{1,0:T(8,128)(2,1)S(1)} %collective-permute-done.4.other_ref, bf16[256,128]{1,0:T(8,128)(2,1)S(1)} %shard_map.50._.near_ref, bf16[256,128]{1,0:T(8,128)(2,1)S(1)} %collective-permute-done.5.far_ref), custom_call_target="tpu_custom_call" | custom-call | tf_op jit(solution)/shard_map/pallas_call | solution.py:226
  (1 shorter events, 0.0 us)
Async XLA Ops:
  3.5 11.6 %collective-permute-start = (bf16[8,128,256]{2,1,0:T(8,128)(2,1)S(1)}, bf16[8,128,256]{2,1,0:T(8,128)(2,1)S(1)}, u32[]{:S(2)}, u32[]{:S(2)}) collective-permute-start(bf16[8,128,256]{2,1,0:T(8,128)(2,1)S(1)} %get-tuple-element.18), channel_id=1, source_target_pairs={{0,16},{1,17},{2,18},{3,19},{4,20},{5,21},{6,22},{7,23},{8,24},{9,... | collective-permute-start | bytes 1572872 | tf_op jit(solution)/shard_map/ppermute | solution.py:255
  15.3 11.1 %collective-permute-start.1 = (bf16[8,128,256]{2,1,0:T(8,128)(2,1)S(1)}, bf16[8,128,256]{2,1,0:T(8,128)(2,1)S(1)}, u32[]{:S(2)}, u32[]{:S(2)}) collective-permute-start(bf16[8,128,256]{2,1,0:T(8,128)(2,1)S(1)} %shard_map.48), channel_id=1, source_target_pairs={{0,64},{1,65},{2,66},{3,67},{4,68},{5,69},{6,70},{7,71},{8,72},{9,... | collective-permute-start | bytes 1572872 | tf_op jit(solution)/shard_map/ppermute | solution.py:261
  17.2 9.2 %collective-permute-start.2 = (bf16[8,128,256]{2,1,0:T(8,128)(2,1)S(1)}, bf16[8,128,256]{2,1,0:T(8,128)(2,1)S(1)}, u32[]{:S(2)}, u32[]{:S(2)}) collective-permute-start(bf16[8,128,256]{2,1,0:T(8,128)(2,1)S(1)} %get-tuple-element.21), channel_id=1, source_target_pairs={{0,16},{1,17},{2,18},{3,19},{4,20},{5,21},{6,22},{7,23},{8,24},{9,... | collective-permute-start | bytes 1572872 | tf_op jit(solution)/shard_map/ppermute | solution.py:255
  19.1 12.1 %collective-permute-start.3 = (bf16[256,128]{1,0:T(8,128)(2,1)S(1)}, bf16[256,128]{1,0:T(8,128)(2,1)S(1)}, u32[]{:S(2)}, u32[]{:S(2)}) collective-permute-start(bf16[256,128]{1,0:T(8,128)(2,1)S(1)} %get-tuple-element.24), channel_id=1, source_target_pairs={{3,104},{6,197},{7,238},{12,394},{13,419},{14,457},{15,482},{20,14... | collective-permute-start | bytes 196616 | tf_op jit(solution)/shard_map/ppermute | solution.py:266
  27.3 21.2 %all-to-all-start = ((bf16[8,128,256]{2,1,0:T(8,128)(2,1)}), bf16[8,128,256]{2,1,0:T(8,128)(2,1)S(1)}, u32[]{:S(2)}, u32[]{:S(2)}) async-start(bf16[8,128,256]{2,1,0:T(8,128)(2,1)} %shard_map.49), calls=%async_computation | async-start | bytes 1048576 | tf_op jit(solution)/shard_map/all_to_all | solution.py:274
  31.2 20.1 %collective-permute-start.5 = (bf16[256,128]{1,0:T(8,128)(2,1)S(1)}, bf16[256,128]{1,0:T(8,128)(2,1)S(1)}, u32[]{:S(2)}, u32[]{:S(2)}) collective-permute-start(bf16[256,128]{1,0:T(8,128)(2,1)S(1)} %get-tuple-element.24), channel_id=1, source_target_pairs={{0,0},{1,41},{2,71},{4,134},{5,175},{8,268},{9,293},{10,331},{11,3... | collective-permute-start | bytes 196616 | tf_op jit(solution)/shard_map/ppermute | solution.py:273
  48.6 3.6 %collective-permute-start.4 = (bf16[128,256]{1,0:T(8,128)(2,1)S(1)}, bf16[128,256]{1,0:T(8,128)(2,1)S(1)}, u32[]{:S(2)}, u32[]{:S(2)}) collective-permute-start(bf16[128,256]{1,0:T(8,128)(2,1)S(1)} %shard_map.51.own_ref), channel_id=1, source_target_pairs={{0,16},{1,17},{2,18},{3,19},{4,20},{5,21},{6,22},{7,23},{8,24},{9,... | collective-permute-start | bytes 196616 | tf_op jit(solution)/shard_map/ppermute | solution.py:255

commit v6 on v5

--- a/solution.py
+++ b/solution.py
@@ -49,7 +49,7 @@
     for tile in range(tiles):
         first = pl.multiple_of((2 * tile + parity) * columns, columns)
         copies.append(pltpu.make_async_copy(act_hbm.at[:, pl.ds(first, columns)], act.at[tile], sems.at[tile]))
-        copies[-1].start()
+        copies[-1].start(priority=1)
 
     def run():
         for tile in range(tiles):
@@ -236,14 +236,14 @@
     out_ref[...] = block_ref[...]
 
 
-def hold(block):
+def hold(block, flops):
     return pl.pallas_call(
         hold_kernel,
         out_shape=jax.ShapeDtypeStruct(block.shape, BF16),
         in_specs=[VMEM],
         out_specs=VMEM,
         compiler_params=pltpu.CompilerParams(vmem_limit_bytes=4 * 2**20),
-        cost_estimate=pl.CostEstimate(flops=5 * 10**10, bytes_accessed=2**17, transcendentals=0),
+        cost_estimate=pl.CostEstimate(flops=flops, bytes_accessed=2**17, transcendentals=0),
     )(block)
 
 
@@ -264,15 +264,14 @@
     send, keep, turned, half = leading(shape, at, activations, out_grads, input_inverse, output_inverse)
     lower, higher = spread(shape)
     near = lax.ppermute(half, AXES, lower)
-    got = to_core(send)
+    send_y, turned = lax.optimization_barrier((first_sum(keep, to_core(send)), turned))
     send, rest = trailing(shape, at, activations, out_grads, turned)
-    send_y, send = lax.optimization_barrier((first_sum(keep, got), send))
-    got_y = to_y(send_y)
+    got_y = hold(to_y(send_y), 5 * 10**9)
     total = second_sum(rest, got_y, to_core(send))
     total, half = lax.optimization_barrier((total, half))
     far = lax.ppermute(half, AXES, higher)
     pieces = lax.all_to_all(total, ("yk", "xh"), 0, 0)
-    near = hold(near)
+    near = hold(near, 5 * 10**10)
     gathered = sum_pieces(pieces, near)
     return right(core, gathered, to_core(gathered), near, far)
 

time: 53.3 us -> 52.1 us (0.977)
  waiting for transfers between devices: 14.1 us -> 13 us
    ppermute x1, waiting for transfers between devices: 6.6 us -> 3.4 us  [to_y(): return lax.ppermute(a, AXES, pairs(shape, move))]
    ppermute x3, waiting for transfers between devices: 0.87 us -> 2.39 us  [to_core(): lax.ppermute(a, AXES, pairs(shape, lambda y, x, c, m: (y, x, 1 - c, m)))]
    all_to_all x1, waiting for transfers between devices: 6.63 us -> 7.19 us  [per_device(): pieces = lax.all_to_all(total, ('yk', 'xh'), 0, 0)]
  transfers between devices with their start and end apart: 7 -> 7, of which waited for: 3 -> 4; matrix products, arithmetic and copies ran while one was open for 0% -> 0% of each run, Pallas kernels for 7% -> 7%
where the time goes in v6:
time: 52.1 us; the launch traced here: 51.7 us
  starting transfers between devices  30.7 us (59%)
  waiting for transfers between devices  13 us (25%)
  Pallas kernels  7.84 us (15%)
    ppermute x3, starting transfers between devices, to_core(): lax.ppermute(a, AXES, pairs(shape, lambda y, x, c, m: (y, x, 1 - c, m)))  13.6 us
    ppermute x1, starting transfers between devices, per_device(): far = lax.ppermute(half, AXES, higher)  10.6 us
    all_to_all x1, waiting for transfers between devices, per_device(): pieces = lax.all_to_all(total, ('yk', 'xh'), 0, 0)  7.19 us
    all_to_all x1, starting transfers between devices, per_device(): pieces = lax.all_to_all(total, ('yk', 'xh'), 0, 0)  3.91 us
    ppermute x1, waiting for transfers between devices, to_y(): return lax.ppermute(a, AXES, pairs(shape, move))  3.4 us
    pallas_call x1, Pallas kernels, leading(): pl.pallas_call(leading_kernel, out_shape=(pltpu.VMEM(blocks, BF16), pltpu...  3.13 us
    pallas_call x1, Pallas kernels, trailing(): pl.pallas_call(trailing_kernel, out_shape=(pltpu.VMEM(blocks, BF16), pltp...  2.83 us
    ppermute x3, waiting for transfers between devices, to_core(): lax.ppermute(a, AXES, pairs(shape, lambda y, x, c, m: (y, x, 1 - c, m)))  2.39 us
  transfers between devices with their start and end apart: 7, of which 4 were waited for; matrix products, arithmetic and copies ran while one was open for 0% of the time, Pallas kernels for 7%

profile of v6, /device:TPU:1, one launch (start us, length us, event | category | flops | bytes accessed | tf_op | source)
XLA Modules:
  0.0 51.7 jit_solution(209130486547731811)
XLA Ops:
  0.0 0.1 pad_add_fusion.at_ref
  0.1 3.1 %shard_map.46 = (bf16[8,128,256]{2,1,0:T(8,128)(2,1)S(1)}, f32[8,128,256]{2,1,0:T(8,128)S(1)}, bf16[256,512]{1,0:T(8,128)(2,1)S(1)}, bf16[256,128]{1,0:T(8,128)(2,1)S(1)}) custom-call(s32[2]{0:T(128)S(1)} %pad_add_fusion.at_ref, bf16[512,256]{1,0:T(8,128)(2,1)} %grads_hbm.1, bf16[256,256]{1,0:T(8,128)(2,1)} %left_hbm.1, bf16[256,256]{1,0:T(8,128)(2,1)} %right_hbm.1, ...), custom_call_target="tpu_custom_call" | custom-call | flops 536870912 | bytes 2097152 | tf_op jit(solution)/shard_map/pallas_call | solution.py:119
  3.2 8.8 %collective-permute-start = (bf16[8,128,256]{2,1,0:T(8,128)(2,1)S(1)}, bf16[8,128,256]{2,1,0:T(8,128)(2,1)S(1)}, u32[]{:S(2)}, u32[]{:S(2)}) collective-permute-start(bf16[8,128,256]{2,1,0:T(8,128)(2,1)S(1)} %get-tuple-element.16), channel_id=1, source_target_pairs={{0,16},{1,17},{2,18},{3,19},{4,20},{5,21},{6,22},{7,23},{8,24},{9,... | collective-permute-start | bytes 1572872 | tf_op jit(solution)/shard_map/ppermute | solution.py:255
  12.0 1.5 %collective-permute-done.got_ref = bf16[8,128,256]{2,1,0:T(8,128)(2,1)S(1)} collective-permute-done((bf16[8,128,256]{2,1,0:T(8,128)(2,1)S(1)}, bf16[8,128,256]{2,1,0:T(8,128)(2,1)S(1)}, u32[]{:S(2)}, u32[]{:S(2)}) %collective-permute-start) | collective-permute-done | bytes 524320 | tf_op jit(solution)/shard_map/ppermute | solution.py:255
  13.5 0.1 shard_map.47
  13.6 1.9 %collective-permute-start.1 = (bf16[8,128,256]{2,1,0:T(8,128)(2,1)S(1)}, bf16[8,128,256]{2,1,0:T(8,128)(2,1)S(1)}, u32[]{:S(2)}, u32[]{:S(2)}) collective-permute-start(bf16[8,128,256]{2,1,0:T(8,128)(2,1)S(1)} %shard_map.47), channel_id=1, source_target_pairs={{0,64},{1,65},{2,66},{3,67},{4,68},{5,69},{6,70},{7,71},{8,72},{9,... | collective-permute-start | bytes 1572872 | tf_op jit(solution)/shard_map/ppermute | solution.py:261
  15.5 2.8 %shard_map.48 = (bf16[8,128,256]{2,1,0:T(8,128)(2,1)S(1)}, f32[8,128,256]{2,1,0:T(8,128)S(1)}) custom-call(s32[2]{0:T(128)S(1)} %pad_add_fusion.at_ref, bf16[256,512]{1,0:T(8,128)(2,1)S(1)} %get-tuple-element.18.turned, bf16[512,4096]{1,0:T(8,128)(2,1)} %act_hbm.3), custom_call_target="tpu_custom_call" | custom-call | flops 536870912 | bytes 2097152 | tf_op jit(solution)/shard_map/pallas_call | solution.py:143
  18.4 2.3 %collective-permute-start.2 = (bf16[8,128,256]{2,1,0:T(8,128)(2,1)S(1)}, bf16[8,128,256]{2,1,0:T(8,128)(2,1)S(1)}, u32[]{:S(2)}, u32[]{:S(2)}) collective-permute-start(bf16[8,128,256]{2,1,0:T(8,128)(2,1)S(1)} %get-tuple-element.21), channel_id=1, source_target_pairs={{0,16},{1,17},{2,18},{3,19},{4,20},{5,21},{6,22},{7,23},{8,24},{9,... | collective-permute-start | bytes 1572872 | tf_op jit(solution)/shard_map/ppermute | solution.py:255
  20.7 0.7 %collective-permute-start.3 = (bf16[256,128]{1,0:T(8,128)(2,1)S(1)}, bf16[256,128]{1,0:T(8,128)(2,1)S(1)}, u32[]{:S(2)}, u32[]{:S(2)}) collective-permute-start(bf16[256,128]{1,0:T(8,128)(2,1)S(1)} %get-tuple-element.24), channel_id=1, source_target_pairs={{3,104},{6,197},{7,238},{12,394},{13,419},{14,457},{15,482},{20,14... | collective-permute-start | bytes 196616 | tf_op jit(solution)/shard_map/ppermute | solution.py:266
  21.3 3.4 %collective-permute-done.1.block_ref = bf16[8,128,256]{2,1,0:T(8,128)(2,1)S(1)} collective-permute-done((bf16[8,128,256]{2,1,0:T(8,128)(2,1)S(1)}, bf16[8,128,256]{2,1,0:T(8,128)(2,1)S(1)}, u32[]{:S(2)}, u32[]{:S(2)}) %collective-permute-start.1) | collective-permute-done | bytes 524320 | tf_op jit(solution)/shard_map/ppermute | solution.py:261
  24.8 0.0 collective-permute-done.2.got_ref
  24.8 0.9 %shard_map.50 = bf16[8,128,256]{2,1,0:T(8,128)(2,1)} custom-call(f32[8,128,256]{2,1,0:T(8,128)S(1)} %get-tuple-element.19.keep_ref, bf16[8,128,256]{2,1,0:T(8,128)(2,1)S(1)} %shard_map.49.more_ref, bf16[8,128,256]{2,1,0:T(8,128)(2,1)S(1)} %collective-permute-done.2.got_ref), custom_call_target="tpu_custom_call" | custom-call | tf_op jit(solution)/shard_map/pallas_call | solution.py:186
  25.7 3.9 %all-to-all-start = ((bf16[8,128,256]{2,1,0:T(8,128)(2,1)}), bf16[8,128,256]{2,1,0:T(8,128)(2,1)S(1)}, u32[]{:S(2)}, u32[]{:S(2)}) async-start(bf16[8,128,256]{2,1,0:T(8,128)(2,1)} %shard_map.50), calls=%async_computation | async-start | bytes 1048576 | tf_op jit(solution)/shard_map/all_to_all | solution.py:273
  29.6 0.0 collective-permute-done.3.block_ref
  29.6 10.6 %collective-permute-start.5 = (bf16[256,128]{1,0:T(8,128)(2,1)S(1)}, bf16[256,128]{1,0:T(8,128)(2,1)S(1)}, u32[]{:S(2)}, u32[]{:S(2)}) collective-permute-start(bf16[256,128]{1,0:T(8,128)(2,1)S(1)} %get-tuple-element.24), channel_id=1, source_target_pairs={{0,0},{1,41},{2,71},{4,134},{5,175},{8,268},{9,293},{10,331},{11,3... | collective-permute-start | bytes 196616 | tf_op jit(solution)/shard_map/ppermute | solution.py:272
  40.3 7.2 %all-to-all-done.pieces_ref = bf16[8,128,256]{2,1,0:T(8,128)(2,1)S(1)} async-done(((bf16[8,128,256]{2,1,0:T(8,128)(2,1)}), bf16[8,128,256]{2,1,0:T(8,128)(2,1)S(1)}, u32[]{:S(2)}, u32[]{:S(2)}) %all-to-all-start) | async-done | bytes 524320 | tf_op jit(solution)/shard_map/all_to_all | solution.py:273
  47.5 0.1 shard_map.52.own_ref
  47.5 2.5 %collective-permute-start.4 = (bf16[128,256]{1,0:T(8,128)(2,1)S(1)}, bf16[128,256]{1,0:T(8,128)(2,1)S(1)}, u32[]{:S(2)}, u32[]{:S(2)}) collective-permute-start(bf16[128,256]{1,0:T(8,128)(2,1)S(1)} %shard_map.52.own_ref), channel_id=1, source_target_pairs={{0,16},{1,17},{2,18},{3,19},{4,20},{5,21},{6,22},{7,23},{8,24},{9,... | collective-permute-start | bytes 196616 | tf_op jit(solution)/shard_map/ppermute | solution.py:255
  50.0 0.0 collective-permute-done.5.far_ref
  50.0 0.9 %collective-permute-done.4.other_ref = bf16[128,256]{1,0:T(8,128)(2,1)S(1)} collective-permute-done((bf16[128,256]{1,0:T(8,128)(2,1)S(1)}, bf16[128,256]{1,0:T(8,128)(2,1)S(1)}, u32[]{:S(2)}, u32[]{:S(2)}) %collective-permute-start.4) | collective-permute-done | bytes 65568 | tf_op jit(solution)/shard_map/ppermute | solution.py:255
  50.9 0.8 %shard_map.53 = bf16[256,128]{1,0:T(8,128)(2,1)} custom-call(s32[1]{0:T(128)} %bitcast.core_ref, bf16[128,256]{1,0:T(8,128)(2,1)S(1)} %shard_map.52.own_ref, bf16[128,256]{1,0:T(8,128)(2,1)S(1)} %collective-permute-done.4.other_ref, bf16[256,128]{1,0:T(8,128)(2,1)S(1)} %shard_map.51._.near_ref, bf16[256,128]{1,0:T(8,128)(2,1)S(1)} %collective-permute-done.5.far_ref), custom_call_target="tpu_custom_call" | custom-call | tf_op jit(solution)/shard_map/pallas_call | solution.py:226
  (2 shorter events, 0.0 us)
Async XLA Ops:
  3.2 10.3 %collective-permute-start = (bf16[8,128,256]{2,1,0:T(8,128)(2,1)S(1)}, bf16[8,128,256]{2,1,0:T(8,128)(2,1)S(1)}, u32[]{:S(2)}, u32[]{:S(2)}) collective-permute-start(bf16[8,128,256]{2,1,0:T(8,128)(2,1)S(1)} %get-tuple-element.16), channel_id=1, source_target_pairs={{0,16},{1,17},{2,18},{3,19},{4,20},{5,21},{6,22},{7,23},{8,24},{9,... | collective-permute-start | bytes 1572872 | tf_op jit(solution)/shard_map/ppermute | solution.py:255
  13.6 11.1 %collective-permute-start.1 = (bf16[8,128,256]{2,1,0:T(8,128)(2,1)S(1)}, bf16[8,128,256]{2,1,0:T(8,128)(2,1)S(1)}, u32[]{:S(2)}, u32[]{:S(2)}) collective-permute-start(bf16[8,128,256]{2,1,0:T(8,128)(2,1)S(1)} %shard_map.47), channel_id=1, source_target_pairs={{0,64},{1,65},{2,66},{3,67},{4,68},{5,69},{6,70},{7,71},{8,72},{9,... | collective-permute-start | bytes 1572872 | tf_op jit(solution)/shard_map/ppermute | solution.py:261
  18.4 6.4 %collective-permute-start.2 = (bf16[8,128,256]{2,1,0:T(8,128)(2,1)S(1)}, bf16[8,128,256]{2,1,0:T(8,128)(2,1)S(1)}, u32[]{:S(2)}, u32[]{:S(2)}) collective-permute-start(bf16[8,128,256]{2,1,0:T(8,128)(2,1)S(1)} %get-tuple-element.21), channel_id=1, source_target_pairs={{0,16},{1,17},{2,18},{3,19},{4,20},{5,21},{6,22},{7,23},{8,24},{9,... | collective-permute-start | bytes 1572872 | tf_op jit(solution)/shard_map/ppermute | solution.py:255
  20.7 8.9 %collective-permute-start.3 = (bf16[256,128]{1,0:T(8,128)(2,1)S(1)}, bf16[256,128]{1,0:T(8,128)(2,1)S(1)}, u32[]{:S(2)}, u32[]{:S(2)}) collective-permute-start(bf16[256,128]{1,0:T(8,128)(2,1)S(1)} %get-tuple-element.24), channel_id=1, source_target_pairs={{3,104},{6,197},{7,238},{12,394},{13,419},{14,457},{15,482},{20,14... | collective-permute-start | bytes 196616 | tf_op jit(solution)/shard_map/ppermute | solution.py:266
  25.7 21.8 %all-to-all-start = ((bf16[8,128,256]{2,1,0:T(8,128)(2,1)}), bf16[8,128,256]{2,1,0:T(8,128)(2,1)S(1)}, u32[]{:S(2)}, u32[]{:S(2)}) async-start(bf16[8,128,256]{2,1,0:T(8,128)(2,1)} %shard_map.50), calls=%async_computation | async-start | bytes 1048576 | tf_op jit(solution)/shard_map/all_to_all | solution.py:273
  29.6 20.4 %collective-permute-start.5 = (bf16[256,128]{1,0:T(8,128)(2,1)S(1)}, bf16[256,128]{1,0:T(8,128)(2,1)S(1)}, u32[]{:S(2)}, u32[]{:S(2)}) collective-permute-start(bf16[256,128]{1,0:T(8,128)(2,1)S(1)} %get-tuple-element.24), channel_id=1, source_target_pairs={{0,0},{1,41},{2,71},{4,134},{5,175},{8,268},{9,293},{10,331},{11,3... | collective-permute-start | bytes 196616 | tf_op jit(solution)/shard_map/ppermute | solution.py:272
  47.5 3.4 %collective-permute-start.4 = (bf16[128,256]{1,0:T(8,128)(2,1)S(1)}, bf16[128,256]{1,0:T(8,128)(2,1)S(1)}, u32[]{:S(2)}, u32[]{:S(2)}) collective-permute-start(bf16[128,256]{1,0:T(8,128)(2,1)S(1)} %shard_map.52.own_ref), channel_id=1, source_target_pairs={{0,16},{1,17},{2,18},{3,19},{4,20},{5,21},{6,22},{7,23},{8,24},{9,... | collective-permute-start | bytes 196616 | tf_op jit(solution)/shard_map/ppermute | solution.py:255

commit v7 on v6

--- a/solution.py
+++ b/solution.py
@@ -28,6 +28,12 @@
     ]
 
 
+def lateness(shape, device):
+    y_n, x_n, c_n, m_n = shape
+    y = device // (x_n * c_n * m_n)
+    return 3 * (device % (m_n // 2)) + 2 * min(y, y_n - y)
+
+
 def spread(shape):
     y_n, x_n, _, m_n = shape
     z_n = m_n // 2
@@ -38,8 +44,8 @@
         return to_y, to_x, c, low * z_n + (m % z_n + 3 * (y - to_y) + c * (z_n // 2)) % z_n
 
     whole = pairs(shape, move)
-    down = [(a, b) for a, b in whole if b % z_n < a % z_n]
-    return down, [pair for pair in whole if pair not in down]
+    lower = [(a, b) for a, b in whole if lateness(shape, a) - lateness(shape, b) >= 1]
+    return lower, [pair for pair in whole if pair not in lower]
 
 
 def products(parity, act_hbm, act, turned, send_ref, keep_ref, sems):
@@ -65,9 +71,9 @@
 
 
 def leading_kernel(
-    at_ref, grads_hbm, left_hbm, right_hbm, act_hbm, send_ref, keep_ref, turned, half_ref, grads, left, act, sems, own
+    core_ref, parity_ref, grads_hbm, left_hbm, right_hbm, act_hbm, send_ref, keep_ref, turned, half_ref, grads, left, act, sems, own
 ):
-    core, parity = at_ref[0], at_ref[1]
+    core, parity = core_ref[0], parity_ref[0]
     half = send_ref.shape[1]
     copies = [
         pltpu.make_async_copy(grads_hbm, grads, own.at[0]),
@@ -94,8 +100,8 @@
     last.wait()
 
 
-def trailing_kernel(at_ref, turned, act_hbm, send_ref, keep_ref, act, sems):
-    products(at_ref[1], act_hbm, act, turned, send_ref, keep_ref, sems)()
+def trailing_kernel(parity_ref, turned, act_hbm, send_ref, keep_ref, act, sems):
+    products(parity_ref[0], act_hbm, act, turned, send_ref, keep_ref, sems)()
 
 
 def sizes(shape, activations, out_grads):
@@ -124,7 +130,7 @@
             pltpu.VMEM(out_grads.shape[::-1], BF16),
             pltpu.VMEM(half, BF16),
         ),
-        in_specs=[SMEM, hbm, hbm, hbm, hbm],
+        in_specs=[SMEM, SMEM, hbm, hbm, hbm, hbm],
         out_specs=(VMEM, VMEM, VMEM, VMEM),
         scratch_shapes=[
             pltpu.VMEM(out_grads.shape, BF16),
@@ -135,7 +141,7 @@
         ],
         compiler_params=pltpu.CompilerParams(vmem_limit_bytes=12 * 2**20),
         cost_estimate=cost,
-    )(at, *operands)
+    )(*at, *operands)
 
 
 def trailing(shape, at, activations, out_grads, turned):
@@ -151,7 +157,7 @@
         ],
         compiler_params=pltpu.CompilerParams(vmem_limit_bytes=12 * 2**20),
         cost_estimate=cost,
-    )(at, turned, pltpu.with_memory_space_constraint(activations, pltpu.HBM))
+    )(at[1], turned, pltpu.with_memory_space_constraint(activations, pltpu.HBM))
 
 
 def first_kernel(keep_ref, got_ref, send_ref):
@@ -260,7 +266,7 @@
 
         return lax.ppermute(a, AXES, pairs(shape, move))
 
-    at = jnp.stack([core, parity])
+    at = core.reshape(1), parity.reshape(1)
     send, keep, turned, half = leading(shape, at, activations, out_grads, input_inverse, output_inverse)
     lower, higher = spread(shape)
     near = lax.ppermute(half, AXES, lower)

time: 52.1 us -> 51.3 us (0.985)
  the two profiles are of different devices: /device:TPU:1 before, /device:TPU:135 now
where the time goes in v7:
time: 51.3 us; the launch traced here: 51 us
  starting transfers between devices  37.2 us (73%)
  waiting for transfers between devices  6.91 us (13%)
  Pallas kernels  6.8 us (13%)
    ppermute x1, starting transfers between devices, per_device(): far = lax.ppermute(half, AXES, higher)  11.9 us
    ppermute x3, starting transfers between devices, to_core(): lax.ppermute(a, AXES, pairs(shape, lambda y, x, c, m: (y, x, 1 - c, m)))  10.5 us
    all_to_all x1, starting transfers between devices, per_device(): pieces = lax.all_to_all(total, ('yk', 'xh'), 0, 0)  8.99 us
    ppermute x1, starting transfers between devices, to_y(): return lax.ppermute(a, AXES, pairs(shape, move))  5.1 us
    all_to_all x1, waiting for transfers between devices, per_device(): pieces = lax.all_to_all(total, ('yk', 'xh'), 0, 0)  2.86 us
    pallas_call x1, Pallas kernels, leading(): pl.pallas_call(leading_kernel, out_shape=(pltpu.VMEM(blocks, BF16), pltpu...  2.62 us
    ppermute x3, waiting for transfers between devices, to_core(): lax.ppermute(a, AXES, pairs(shape, lambda y, x, c, m: (y, x, 1 - c, m)))  2.39 us
    pallas_call x1, Pallas kernels, trailing(): pl.pallas_call(trailing_kernel, out_shape=(pltpu.VMEM(blocks, BF16), pltp...  2.29 us
  transfers between devices with their start and end apart: 7, of which 4 were waited for; matrix products, arithmetic and copies ran while one was open for 0% of the time, Pallas kernels for 6%

profile of v7, /device:TPU:135, one launch (start us, length us, event | category | flops | bytes accessed | tf_op | source)
XLA Modules:
  0.0 51.0 jit_solution(11030660181855157180)
XLA Ops:
  0.0 2.6 %shard_map.46 = (bf16[8,128,256]{2,1,0:T(8,128)(2,1)S(1)}, f32[8,128,256]{2,1,0:T(8,128)S(1)}, bf16[256,512]{1,0:T(8,128)(2,1)S(1)}, bf16[256,128]{1,0:T(8,128)(2,1)S(1)}) custom-call(s32[1]{0:T(128)} %bitcast.core_ref, s32[1]{0:T(128)} %bitcast.1.parity_ref, bf16[512,256]{1,0:T(8,128)(2,1)} %grads_hbm.1, bf16[256,256]{1,0:T(8,128)(2,1)} %left_hbm.1, ...), custom_call_target="tpu_custom_call" | custom-call | flops 536870912 | bytes 2097152 | tf_op jit(solution)/shard_map/pallas_call | solution.py:125
  2.6 2.6 %collective-permute-start = (bf16[8,128,256]{2,1,0:T(8,128)(2,1)S(1)}, bf16[8,128,256]{2,1,0:T(8,128)(2,1)S(1)}, u32[]{:S(2)}, u32[]{:S(2)}) collective-permute-start(bf16[8,128,256]{2,1,0:T(8,128)(2,1)S(1)} %get-tuple-element.16), channel_id=1, source_target_pairs={{0,16},{1,17},{2,18},{3,19},{4,20},{5,21},{6,22},{7,23},{8,24},{9,... | collective-permute-start | bytes 1572872 | tf_op jit(solution)/shard_map/ppermute | solution.py:261
  5.2 1.5 %collective-permute-done.got_ref = bf16[8,128,256]{2,1,0:T(8,128)(2,1)S(1)} collective-permute-done((bf16[8,128,256]{2,1,0:T(8,128)(2,1)S(1)}, bf16[8,128,256]{2,1,0:T(8,128)(2,1)S(1)}, u32[]{:S(2)}, u32[]{:S(2)}) %collective-permute-start) | collective-permute-done | bytes 524320 | tf_op jit(solution)/shard_map/ppermute | solution.py:261
  6.7 0.1 shard_map.47
  6.8 5.1 %collective-permute-start.1 = (bf16[8,128,256]{2,1,0:T(8,128)(2,1)S(1)}, bf16[8,128,256]{2,1,0:T(8,128)(2,1)S(1)}, u32[]{:S(2)}, u32[]{:S(2)}) collective-permute-start(bf16[8,128,256]{2,1,0:T(8,128)(2,1)S(1)} %shard_map.47), channel_id=1, source_target_pairs={{0,64},{1,65},{2,66},{3,67},{4,68},{5,69},{6,70},{7,71},{8,72},{9,... | collective-permute-start | bytes 1572872 | tf_op jit(solution)/shard_map/ppermute | solution.py:267
  11.9 2.3 %shard_map.48 = (bf16[8,128,256]{2,1,0:T(8,128)(2,1)S(1)}, f32[8,128,256]{2,1,0:T(8,128)S(1)}) custom-call(s32[1]{0:T(128)} %bitcast.1.parity_ref, bf16[256,512]{1,0:T(8,128)(2,1)S(1)} %get-tuple-element.18.turned, bf16[512,4096]{1,0:T(8,128)(2,1)} %act_hbm.3), custom_call_target="tpu_custom_call" | custom-call | flops 536870912 | bytes 2097152 | tf_op jit(solution)/shard_map/pallas_call | solution.py:149
  14.2 1.9 %collective-permute-start.2 = (bf16[8,128,256]{2,1,0:T(8,128)(2,1)S(1)}, bf16[8,128,256]{2,1,0:T(8,128)(2,1)S(1)}, u32[]{:S(2)}, u32[]{:S(2)}) collective-permute-start(bf16[8,128,256]{2,1,0:T(8,128)(2,1)S(1)} %get-tuple-element.21), channel_id=1, source_target_pairs={{0,16},{1,17},{2,18},{3,19},{4,20},{5,21},{6,22},{7,23},{8,24},{9,... | collective-permute-start | bytes 1572872 | tf_op jit(solution)/shard_map/ppermute | solution.py:261
  16.2 0.7 %collective-permute-start.3 = (bf16[256,128]{1,0:T(8,128)(2,1)S(1)}, bf16[256,128]{1,0:T(8,128)(2,1)S(1)}, u32[]{:S(2)}, u32[]{:S(2)}) collective-permute-start(bf16[256,128]{1,0:T(8,128)(2,1)S(1)} %get-tuple-element.24), channel_id=1, source_target_pairs={{3,104},{12,394},{13,419},{14,457},{15,482},{20,146},{21,187},{22,... | collective-permute-start | bytes 196616 | tf_op jit(solution)/shard_map/ppermute | solution.py:272
  16.8 1.7 %collective-permute-done.1.block_ref = bf16[8,128,256]{2,1,0:T(8,128)(2,1)S(1)} collective-permute-done((bf16[8,128,256]{2,1,0:T(8,128)(2,1)S(1)}, bf16[8,128,256]{2,1,0:T(8,128)(2,1)S(1)}, u32[]{:S(2)}, u32[]{:S(2)}) %collective-permute-start.1) | collective-permute-done | bytes 524320 | tf_op jit(solution)/shard_map/ppermute | solution.py:267
  18.5 0.0 collective-permute-done.2.got_ref
  18.5 0.9 %shard_map.50 = bf16[8,128,256]{2,1,0:T(8,128)(2,1)} custom-call(f32[8,128,256]{2,1,0:T(8,128)S(1)} %get-tuple-element.19.keep_ref, bf16[8,128,256]{2,1,0:T(8,128)(2,1)S(1)} %shard_map.49.more_ref, bf16[8,128,256]{2,1,0:T(8,128)(2,1)S(1)} %collective-permute-done.2.got_ref), custom_call_target="tpu_custom_call" | custom-call | tf_op jit(solution)/shard_map/pallas_call | solution.py:192
  19.4 9.0 %all-to-all-start = ((bf16[8,128,256]{2,1,0:T(8,128)(2,1)}), bf16[8,128,256]{2,1,0:T(8,128)(2,1)S(1)}, u32[]{:S(2)}, u32[]{:S(2)}) async-start(bf16[8,128,256]{2,1,0:T(8,128)(2,1)} %shard_map.50), calls=%async_computation | async-start | bytes 1048576 | tf_op jit(solution)/shard_map/all_to_all | solution.py:279
  28.4 0.0 collective-permute-done.3.block_ref
  28.4 11.9 %collective-permute-start.5 = (bf16[256,128]{1,0:T(8,128)(2,1)S(1)}, bf16[256,128]{1,0:T(8,128)(2,1)S(1)}, u32[]{:S(2)}, u32[]{:S(2)}) collective-permute-start(bf16[256,128]{1,0:T(8,128)(2,1)S(1)} %get-tuple-element.24), channel_id=1, source_target_pairs={{0,0},{1,41},{2,71},{4,134},{5,175},{6,197},{7,238},{8,268},{9,293... | collective-permute-start | bytes 196616 | tf_op jit(solution)/shard_map/ppermute | solution.py:278
  40.4 2.9 %all-to-all-done.pieces_ref = bf16[8,128,256]{2,1,0:T(8,128)(2,1)S(1)} async-done(((bf16[8,128,256]{2,1,0:T(8,128)(2,1)}), bf16[8,128,256]{2,1,0:T(8,128)(2,1)S(1)}, u32[]{:S(2)}, u32[]{:S(2)}) %all-to-all-start) | async-done | bytes 524320 | tf_op jit(solution)/shard_map/all_to_all | solution.py:279
  43.2 0.1 shard_map.52.own_ref
  43.3 6.0 %collective-permute-start.4 = (bf16[128,256]{1,0:T(8,128)(2,1)S(1)}, bf16[128,256]{1,0:T(8,128)(2,1)S(1)}, u32[]{:S(2)}, u32[]{:S(2)}) collective-permute-start(bf16[128,256]{1,0:T(8,128)(2,1)S(1)} %shard_map.52.own_ref), channel_id=1, source_target_pairs={{0,16},{1,17},{2,18},{3,19},{4,20},{5,21},{6,22},{7,23},{8,24},{9,... | collective-permute-start | bytes 196616 | tf_op jit(solution)/shard_map/ppermute | solution.py:261
  49.3 0.0 collective-permute-done.5.far_ref
  49.3 0.9 %collective-permute-done.4.other_ref = bf16[128,256]{1,0:T(8,128)(2,1)S(1)} collective-permute-done((bf16[128,256]{1,0:T(8,128)(2,1)S(1)}, bf16[128,256]{1,0:T(8,128)(2,1)S(1)}, u32[]{:S(2)}, u32[]{:S(2)}) %collective-permute-start.4) | collective-permute-done | bytes 65568 | tf_op jit(solution)/shard_map/ppermute | solution.py:261
  50.2 0.8 %shard_map.53 = bf16[256,128]{1,0:T(8,128)(2,1)} custom-call(s32[1]{0:T(128)} %bitcast.core_ref, bf16[128,256]{1,0:T(8,128)(2,1)S(1)} %shard_map.52.own_ref, bf16[128,256]{1,0:T(8,128)(2,1)S(1)} %collective-permute-done.4.other_ref, bf16[256,128]{1,0:T(8,128)(2,1)S(1)} %shard_map.51._.near_ref, bf16[256,128]{1,0:T(8,128)(2,1)S(1)} %collective-permute-done.5.far_ref), custom_call_target="tpu_custom_call" | custom-call | tf_op jit(solution)/shard_map/pallas_call | solution.py:232
  (2 shorter events, 0.0 us)
Async XLA Ops:
  2.6 4.1 %collective-permute-start = (bf16[8,128,256]{2,1,0:T(8,128)(2,1)S(1)}, bf16[8,128,256]{2,1,0:T(8,128)(2,1)S(1)}, u32[]{:S(2)}, u32[]{:S(2)}) collective-permute-start(bf16[8,128,256]{2,1,0:T(8,128)(2,1)S(1)} %get-tuple-element.16), channel_id=1, source_target_pairs={{0,16},{1,17},{2,18},{3,19},{4,20},{5,21},{6,22},{7,23},{8,24},{9,... | collective-permute-start | bytes 1572872 | tf_op jit(solution)/shard_map/ppermute | solution.py:261
  6.8 11.7 %collective-permute-start.1 = (bf16[8,128,256]{2,1,0:T(8,128)(2,1)S(1)}, bf16[8,128,256]{2,1,0:T(8,128)(2,1)S(1)}, u32[]{:S(2)}, u32[]{:S(2)}) collective-permute-start(bf16[8,128,256]{2,1,0:T(8,128)(2,1)S(1)} %shard_map.47), channel_id=1, source_target_pairs={{0,64},{1,65},{2,66},{3,67},{4,68},{5,69},{6,70},{7,71},{8,72},{9,... | collective-permute-start | bytes 1572872 | tf_op jit(solution)/shard_map/ppermute | solution.py:267
  14.2 4.3 %collective-permute-start.2 = (bf16[8,128,256]{2,1,0:T(8,128)(2,1)S(1)}, bf16[8,128,256]{2,1,0:T(8,128)(2,1)S(1)}, u32[]{:S(2)}, u32[]{:S(2)}) collective-permute-start(bf16[8,128,256]{2,1,0:T(8,128)(2,1)S(1)} %get-tuple-element.21), channel_id=1, source_target_pairs={{0,16},{1,17},{2,18},{3,19},{4,20},{5,21},{6,22},{7,23},{8,24},{9,... | collective-permute-start | bytes 1572872 | tf_op jit(solution)/shard_map/ppermute | solution.py:261
  16.2 12.3 %collective-permute-start.3 = (bf16[256,128]{1,0:T(8,128)(2,1)S(1)}, bf16[256,128]{1,0:T(8,128)(2,1)S(1)}, u32[]{:S(2)}, u32[]{:S(2)}) collective-permute-start(bf16[256,128]{1,0:T(8,128)(2,1)S(1)} %get-tuple-element.24), channel_id=1, source_target_pairs={{3,104},{12,394},{13,419},{14,457},{15,482},{20,146},{21,187},{22,... | collective-permute-start | bytes 196616 | tf_op jit(solution)/shard_map/ppermute | solution.py:272
  19.4 23.8 %all-to-all-start = ((bf16[8,128,256]{2,1,0:T(8,128)(2,1)}), bf16[8,128,256]{2,1,0:T(8,128)(2,1)S(1)}, u32[]{:S(2)}, u32[]{:S(2)}) async-start(bf16[8,128,256]{2,1,0:T(8,128)(2,1)} %shard_map.50), calls=%async_computation | async-start | bytes 1048576 | tf_op jit(solution)/shard_map/all_to_all | solution.py:279
  28.4 20.9 %collective-permute-start.5 = (bf16[256,128]{1,0:T(8,128)(2,1)S(1)}, bf16[256,128]{1,0:T(8,128)(2,1)S(1)}, u32[]{:S(2)}, u32[]{:S(2)}) collective-permute-start(bf16[256,128]{1,0:T(8,128)(2,1)S(1)} %get-tuple-element.24), channel_id=1, source_target_pairs={{0,0},{1,41},{2,71},{4,134},{5,175},{6,197},{7,238},{8,268},{9,293... | collective-permute-start | bytes 196616 | tf_op jit(solution)/shard_map/ppermute | solution.py:278
  43.3 6.9 %collective-permute-start.4 = (bf16[128,256]{1,0:T(8,128)(2,1)S(1)}, bf16[128,256]{1,0:T(8,128)(2,1)S(1)}, u32[]{:S(2)}, u32[]{:S(2)}) collective-permute-start(bf16[128,256]{1,0:T(8,128)(2,1)S(1)} %shard_map.52.own_ref), channel_id=1, source_target_pairs={{0,16},{1,17},{2,18},{3,19},{4,20},{5,21},{6,22},{7,23},{8,24},{9,... | collective-permute-start | bytes 196616 | tf_op jit(solution)/shard_map/ppermute | solution.py:261

commit v8 on v7

--- a/solution.py
+++ b/solution.py
@@ -31,7 +31,8 @@
 def lateness(shape, device):
     y_n, x_n, c_n, m_n = shape
     y = device // (x_n * c_n * m_n)
-    return 3 * (device % (m_n // 2)) + 2 * min(y, y_n - y)
+    x = 2 * (device // (c_n * m_n) % x_n) + device % m_n // (m_n // 2)
+    return 3 * (device % (m_n // 2)) + 2 * min(y, y_n - y) + x
 
 
 def spread(shape):
@@ -180,10 +181,8 @@
     for block in range(keep_ref.shape[0]):
         total = keep_ref[block] + got_ref[block].astype(F32) + more_ref[block].astype(F32)
         total_ref[block] = total.astype(BF16)
-        if block % 2:
-            pair = pl.ds(block - 1, 2)
-            copies.append(pltpu.make_async_copy(total_ref.at[pair], total_hbm.at[pair], sems.at[block // 2]))
-            copies[-1].start()
+        copies.append(pltpu.make_async_copy(total_ref.at[block], total_hbm.at[block], sems.at[block]))
+        copies[-1].start(priority=block % 2)
     for copy in copies:
         copy.wait()
 
@@ -194,7 +193,7 @@
         out_shape=pltpu.HBM(got.shape, BF16),
         in_specs=[VMEM, VMEM, VMEM],
         out_specs=pl.BlockSpec(memory_space=pl.ANY),
-        scratch_shapes=[pltpu.VMEM(got.shape, BF16), pltpu.SemaphoreType.DMA((got.shape[0] // 2,))],
+        scratch_shapes=[pltpu.VMEM(got.shape, BF16), pltpu.SemaphoreType.DMA((got.shape[0],))],
         compiler_params=pltpu.CompilerParams(vmem_limit_bytes=8 * 2**20),
     )(keep, more, got)
 
@@ -239,7 +238,8 @@
 
 
 def hold_kernel(block_ref, out_ref):
-    out_ref[...] = block_ref[...]
+    rows = 16 if len(out_ref.shape) == 2 else 1
+    out_ref[:rows] = block_ref[:rows]
 
 
 def hold(block, flops):
@@ -248,6 +248,7 @@
         out_shape=jax.ShapeDtypeStruct(block.shape, BF16),
         in_specs=[VMEM],
         out_specs=VMEM,
+        input_output_aliases={0: 0},
         compiler_params=pltpu.CompilerParams(vmem_limit_bytes=4 * 2**20),
         cost_estimate=pl.CostEstimate(flops=flops, bytes_accessed=2**17, transcendentals=0),
     )(block)

time: 51.3 us -> 51.3 us (level)
  the two profiles are of different devices: /device:TPU:135 before, /device:TPU:199 now
where the time goes in v8:
time: 51.3 us; the launch traced here: 51 us
  starting transfers between devices  27.9 us (54%)
  waiting for transfers between devices  16.2 us (32%)
  Pallas kernels  6.78 us (13%)
    all_to_all x1, waiting for transfers between devices, per_device(): pieces = lax.all_to_all(total, ('yk', 'xh'), 0, 0)  13.8 us
    ppermute x3, starting transfers between devices, to_core(): lax.ppermute(a, AXES, pairs(shape, lambda y, x, c, m: (y, x, 1 - c, m)))  10.2 us
    all_to_all x1, starting transfers between devices, per_device(): pieces = lax.all_to_all(total, ('yk', 'xh'), 0, 0)  8.84 us
    ppermute x1, starting transfers between devices, to_y(): return lax.ppermute(a, AXES, pairs(shape, move))  5.09 us
    pallas_call x1, Pallas kernels, leading(): pl.pallas_call(leading_kernel, out_shape=(pltpu.VMEM(blocks, BF16), pltpu...  2.62 us
    ppermute x1, starting transfers between devices, per_device(): near = lax.ppermute(half, AXES, lower)  2.46 us
    ppermute x3, waiting for transfers between devices, to_core(): lax.ppermute(a, AXES, pairs(shape, lambda y, x, c, m: (y, x, 1 - c, m)))  2.39 us
    pallas_call x1, Pallas kernels, trailing(): pl.pallas_call(trailing_kernel, out_shape=(pltpu.VMEM(blocks, BF16), pltp...  2.29 us
  transfers between devices with their start and end apart: 7, of which 3 were waited for; matrix products, arithmetic and copies ran while one was open for 0% of the time, Pallas kernels for 6%

profile of v8, /device:TPU:199, one launch (start us, length us, event | category | flops | bytes accessed | tf_op | source)
XLA Modules:
  0.0 51.0 jit_solution(9790838209507596547)
XLA Ops:
  0.0 2.6 %shard_map.46 = (bf16[8,128,256]{2,1,0:T(8,128)(2,1)S(1)}, f32[8,128,256]{2,1,0:T(8,128)S(1)}, bf16[256,512]{1,0:T(8,128)(2,1)S(1)}, bf16[256,128]{1,0:T(8,128)(2,1)S(1)}) custom-call(s32[1]{0:T(128)} %bitcast.core_ref, s32[1]{0:T(128)} %bitcast.1.parity_ref, bf16[512,256]{1,0:T(8,128)(2,1)} %grads_hbm.1, bf16[256,256]{1,0:T(8,128)(2,1)} %left_hbm.1, ...), custom_call_target="tpu_custom_call" | custom-call | flops 536870912 | bytes 2097152 | tf_op jit(solution)/shard_map/pallas_call | solution.py:126
  2.6 2.6 %collective-permute-start = (bf16[8,128,256]{2,1,0:T(8,128)(2,1)S(1)}, bf16[8,128,256]{2,1,0:T(8,128)(2,1)S(1)}, u32[]{:S(2)}, u32[]{:S(2)}) collective-permute-start(bf16[8,128,256]{2,1,0:T(8,128)(2,1)S(1)} %get-tuple-element.16), channel_id=1, source_target_pairs={{0,16},{1,17},{2,18},{3,19},{4,20},{5,21},{6,22},{7,23},{8,24},{9,... | collective-permute-start | bytes 1572872 | tf_op jit(solution)/shard_map/ppermute | solution.py:262
  5.2 1.5 %collective-permute-done.got_ref = bf16[8,128,256]{2,1,0:T(8,128)(2,1)S(1)} collective-permute-done((bf16[8,128,256]{2,1,0:T(8,128)(2,1)S(1)}, bf16[8,128,256]{2,1,0:T(8,128)(2,1)S(1)}, u32[]{:S(2)}, u32[]{:S(2)}) %collective-permute-start) | collective-permute-done | bytes 524320 | tf_op jit(solution)/shard_map/ppermute | solution.py:262
  6.7 0.1 shard_map.47
  6.8 5.1 %collective-permute-start.1 = (bf16[8,128,256]{2,1,0:T(8,128)(2,1)S(1)}, bf16[8,128,256]{2,1,0:T(8,128)(2,1)S(1)}, u32[]{:S(2)}, u32[]{:S(2)}) collective-permute-start(bf16[8,128,256]{2,1,0:T(8,128)(2,1)S(1)} %shard_map.47), channel_id=1, source_target_pairs={{0,64},{1,65},{2,66},{3,67},{4,68},{5,69},{6,70},{7,71},{8,72},{9,... | collective-permute-start | bytes 1572872 | tf_op jit(solution)/shard_map/ppermute | solution.py:268
  11.9 2.3 %shard_map.48 = (bf16[8,128,256]{2,1,0:T(8,128)(2,1)S(1)}, f32[8,128,256]{2,1,0:T(8,128)S(1)}) custom-call(s32[1]{0:T(128)} %bitcast.1.parity_ref, bf16[256,512]{1,0:T(8,128)(2,1)S(1)} %get-tuple-element.18.turned, bf16[512,4096]{1,0:T(8,128)(2,1)} %act_hbm.3), custom_call_target="tpu_custom_call" | custom-call | flops 536870912 | bytes 2097152 | tf_op jit(solution)/shard_map/pallas_call | solution.py:150
  14.2 1.9 %collective-permute-start.2 = (bf16[8,128,256]{2,1,0:T(8,128)(2,1)S(1)}, bf16[8,128,256]{2,1,0:T(8,128)(2,1)S(1)}, u32[]{:S(2)}, u32[]{:S(2)}) collective-permute-start(bf16[8,128,256]{2,1,0:T(8,128)(2,1)S(1)} %get-tuple-element.21), channel_id=1, source_target_pairs={{0,16},{1,17},{2,18},{3,19},{4,20},{5,21},{6,22},{7,23},{8,24},{9,... | collective-permute-start | bytes 1572872 | tf_op jit(solution)/shard_map/ppermute | solution.py:262
  16.2 2.5 %collective-permute-start.3 = (bf16[256,128]{1,0:T(8,128)(2,1)S(1)}, bf16[256,128]{1,0:T(8,128)(2,1)S(1)}, u32[]{:S(2)}, u32[]{:S(2)}) collective-permute-start(bf16[256,128]{1,0:T(8,128)(2,1)S(1)} %get-tuple-element.24), channel_id=1, source_target_pairs={{3,104},{12,394},{13,419},{14,457},{15,482},{20,146},{22,209},{23,... | collective-permute-start | bytes 196616 | tf_op jit(solution)/shard_map/ppermute | solution.py:273
  18.6 0.0 collective-permute-done.1.block_ref
  18.7 0.0 collective-permute-done.2.got_ref
  18.7 0.9 %shard_map.50 = bf16[8,128,256]{2,1,0:T(8,128)(2,1)} custom-call(f32[8,128,256]{2,1,0:T(8,128)S(1)} %get-tuple-element.19.keep_ref, bf16[8,128,256]{2,1,0:T(8,128)(2,1)S(1)} %shard_map.49.more_ref, bf16[8,128,256]{2,1,0:T(8,128)(2,1)S(1)} %collective-permute-done.2.got_ref), custom_call_target="tpu_custom_call" | custom-call | tf_op jit(solution)/shard_map/pallas_call | solution.py:191
  19.6 8.8 %all-to-all-start = ((bf16[8,128,256]{2,1,0:T(8,128)(2,1)}), bf16[8,128,256]{2,1,0:T(8,128)(2,1)S(1)}, u32[]{:S(2)}, u32[]{:S(2)}) async-start(bf16[8,128,256]{2,1,0:T(8,128)(2,1)} %shard_map.50), calls=%async_computation | async-start | bytes 1048576 | tf_op jit(solution)/shard_map/all_to_all | solution.py:280
  28.4 0.0 collective-permute-done.3.block_ref
  28.4 1.3 %collective-permute-start.5 = (bf16[256,128]{1,0:T(8,128)(2,1)S(1)}, bf16[256,128]{1,0:T(8,128)(2,1)S(1)}, u32[]{:S(2)}, u32[]{:S(2)}) collective-permute-start(bf16[256,128]{1,0:T(8,128)(2,1)S(1)} %get-tuple-element.24), channel_id=1, source_target_pairs={{0,0},{1,41},{2,71},{4,134},{5,175},{6,197},{7,238},{8,268},{9,293... | collective-permute-start | bytes 196616 | tf_op jit(solution)/shard_map/ppermute | solution.py:279
  29.7 13.8 %all-to-all-done.pieces_ref = bf16[8,128,256]{2,1,0:T(8,128)(2,1)S(1)} async-done(((bf16[8,128,256]{2,1,0:T(8,128)(2,1)}), bf16[8,128,256]{2,1,0:T(8,128)(2,1)S(1)}, u32[]{:S(2)}, u32[]{:S(2)}) %all-to-all-start) | async-done | bytes 524320 | tf_op jit(solution)/shard_map/all_to_all | solution.py:280
  43.5 0.1 shard_map.52.own_ref
  43.6 5.7 %collective-permute-start.4 = (bf16[128,256]{1,0:T(8,128)(2,1)S(1)}, bf16[128,256]{1,0:T(8,128)(2,1)S(1)}, u32[]{:S(2)}, u32[]{:S(2)}) collective-permute-start(bf16[128,256]{1,0:T(8,128)(2,1)S(1)} %shard_map.52.own_ref), channel_id=1, source_target_pairs={{0,16},{1,17},{2,18},{3,19},{4,20},{5,21},{6,22},{7,23},{8,24},{9,... | collective-permute-start | bytes 196616 | tf_op jit(solution)/shard_map/ppermute | solution.py:262
  49.3 0.0 collective-permute-done.5.far_ref
  49.3 0.9 %collective-permute-done.4.other_ref = bf16[128,256]{1,0:T(8,128)(2,1)S(1)} collective-permute-done((bf16[128,256]{1,0:T(8,128)(2,1)S(1)}, bf16[128,256]{1,0:T(8,128)(2,1)S(1)}, u32[]{:S(2)}, u32[]{:S(2)}) %collective-permute-start.4) | collective-permute-done | bytes 65568 | tf_op jit(solution)/shard_map/ppermute | solution.py:262
  50.2 0.8 %shard_map.53 = bf16[256,128]{1,0:T(8,128)(2,1)} custom-call(s32[1]{0:T(128)} %bitcast.core_ref, bf16[128,256]{1,0:T(8,128)(2,1)S(1)} %shard_map.52.own_ref, bf16[128,256]{1,0:T(8,128)(2,1)S(1)} %collective-permute-done.4.other_ref, bf16[256,128]{1,0:T(8,128)(2,1)S(1)} %shard_map.51._.near_ref, bf16[256,128]{1,0:T(8,128)(2,1)S(1)} %collective-permute-done.5.far_ref), custom_call_target="tpu_custom_call" | custom-call | tf_op jit(solution)/shard_map/pallas_call | solution.py:231
  (2 shorter events, 0.0 us)
Async XLA Ops:
  2.6 4.1 %collective-permute-start = (bf16[8,128,256]{2,1,0:T(8,128)(2,1)S(1)}, bf16[8,128,256]{2,1,0:T(8,128)(2,1)S(1)}, u32[]{:S(2)}, u32[]{:S(2)}) collective-permute-start(bf16[8,128,256]{2,1,0:T(8,128)(2,1)S(1)} %get-tuple-element.16), channel_id=1, source_target_pairs={{0,16},{1,17},{2,18},{3,19},{4,20},{5,21},{6,22},{7,23},{8,24},{9,... | collective-permute-start | bytes 1572872 | tf_op jit(solution)/shard_map/ppermute | solution.py:262
  6.8 11.8 %collective-permute-start.1 = (bf16[8,128,256]{2,1,0:T(8,128)(2,1)S(1)}, bf16[8,128,256]{2,1,0:T(8,128)(2,1)S(1)}, u32[]{:S(2)}, u32[]{:S(2)}) collective-permute-start(bf16[8,128,256]{2,1,0:T(8,128)(2,1)S(1)} %shard_map.47), channel_id=1, source_target_pairs={{0,64},{1,65},{2,66},{3,67},{4,68},{5,69},{6,70},{7,71},{8,72},{9,... | collective-permute-start | bytes 1572872 | tf_op jit(solution)/shard_map/ppermute | solution.py:268
  14.2 4.4 %collective-permute-start.2 = (bf16[8,128,256]{2,1,0:T(8,128)(2,1)S(1)}, bf16[8,128,256]{2,1,0:T(8,128)(2,1)S(1)}, u32[]{:S(2)}, u32[]{:S(2)}) collective-permute-start(bf16[8,128,256]{2,1,0:T(8,128)(2,1)S(1)} %get-tuple-element.21), channel_id=1, source_target_pairs={{0,16},{1,17},{2,18},{3,19},{4,20},{5,21},{6,22},{7,23},{8,24},{9,... | collective-permute-start | bytes 1572872 | tf_op jit(solution)/shard_map/ppermute | solution.py:262
  16.2 12.3 %collective-permute-start.3 = (bf16[256,128]{1,0:T(8,128)(2,1)S(1)}, bf16[256,128]{1,0:T(8,128)(2,1)S(1)}, u32[]{:S(2)}, u32[]{:S(2)}) collective-permute-start(bf16[256,128]{1,0:T(8,128)(2,1)S(1)} %get-tuple-element.24), channel_id=1, source_target_pairs={{3,104},{12,394},{13,419},{14,457},{15,482},{20,146},{22,209},{23,... | collective-permute-start | bytes 196616 | tf_op jit(solution)/shard_map/ppermute | solution.py:273
  19.6 23.9 %all-to-all-start = ((bf16[8,128,256]{2,1,0:T(8,128)(2,1)}), bf16[8,128,256]{2,1,0:T(8,128)(2,1)S(1)}, u32[]{:S(2)}, u32[]{:S(2)}) async-start(bf16[8,128,256]{2,1,0:T(8,128)(2,1)} %shard_map.50), calls=%async_computation | async-start | bytes 1048576 | tf_op jit(solution)/shard_map/all_to_all | solution.py:280
  28.4 20.9 %collective-permute-start.5 = (bf16[256,128]{1,0:T(8,128)(2,1)S(1)}, bf16[256,128]{1,0:T(8,128)(2,1)S(1)}, u32[]{:S(2)}, u32[]{:S(2)}) collective-permute-start(bf16[256,128]{1,0:T(8,128)(2,1)S(1)} %get-tuple-element.24), channel_id=1, source_target_pairs={{0,0},{1,41},{2,71},{4,134},{5,175},{6,197},{7,238},{8,268},{9,293... | collective-permute-start | bytes 196616 | tf_op jit(solution)/shard_map/ppermute | solution.py:279
  43.6 6.6 %collective-permute-start.4 = (bf16[128,256]{1,0:T(8,128)(2,1)S(1)}, bf16[128,256]{1,0:T(8,128)(2,1)S(1)}, u32[]{:S(2)}, u32[]{:S(2)}) collective-permute-start(bf16[128,256]{1,0:T(8,128)(2,1)S(1)} %shard_map.52.own_ref), channel_id=1, source_target_pairs={{0,16},{1,17},{2,18},{3,19},{4,20},{5,21},{6,22},{7,23},{8,24},{9,... | collective-permute-start | bytes 196616 | tf_op jit(solution)/shard_map/ppermute | solution.py:262

commit v9 on v8

--- a/solution.py
+++ b/solution.py
@@ -215,15 +215,30 @@
     )(pieces, held)
 
 
-def right_kernel(core_ref, own_ref, other_ref, near_ref, far_ref, out_ref):
-    half = own_ref.shape[0]
+def own_kernel(own_ref, near_ref, far_ref, out_ref):
+    block = near_ref[...] + far_ref[...]
+    out_ref[...] = jnp.dot(own_ref[...], block, preferred_element_type=F32).astype(BF16)
+
+
+def own_right(own, near, far):
+    return pl.pallas_call(
+        own_kernel,
+        out_shape=jax.ShapeDtypeStruct((own.shape[0], near.shape[1]), BF16),
+        in_specs=[VMEM, VMEM, VMEM],
+        out_specs=VMEM,
+        compiler_params=pltpu.CompilerParams(vmem_limit_bytes=8 * 2**20),
+    )(own, near, far)
+
+
+def right_kernel(core_ref, done_ref, other_ref, near_ref, far_ref, out_ref):
+    half = done_ref.shape[0]
     core = core_ref[0]
+    out_ref[pl.ds(pl.multiple_of(core * half, half), half)] = done_ref[...]
     block = near_ref[...] + far_ref[...]
-    for ref, index in ((own_ref, core), (other_ref, 1 - core)):
-        first = pl.multiple_of(index * half, half)
-        out_ref[pl.ds(first, half)] = jnp.dot(
-            ref[...], block, preferred_element_type=F32
-        ).astype(BF16)
+    first = pl.multiple_of((1 - core) * half, half)
+    out_ref[pl.ds(first, half)] = jnp.dot(
+        other_ref[...], block, preferred_element_type=F32
+    ).astype(BF16)
 
 
 def right(core, own, other, near, far):
@@ -234,7 +249,7 @@
         in_specs=[SMEM, VMEM, VMEM, VMEM, VMEM],
         out_specs=VMEM,
         compiler_params=pltpu.CompilerParams(vmem_limit_bytes=8 * 2**20),
-    )(core.reshape(1), own, other, near, far)
+    )(core.reshape(1), own_right(own, near, far), other, near, far)
 
 
 def hold_kernel(block_ref, out_ref):

time: 51.3 us -> 51.3 us (level)
  transfers between devices with their start and end apart: 7 -> 7, of which waited for: 3 -> 3; matrix products, arithmetic and copies ran while one was open for 0% -> 0% of each run, Pallas kernels for 6% -> 7%
where the time goes in v9:
time: 51.3 us; the launch traced here: 50.9 us
  starting transfers between devices  27.9 us (54%)
  waiting for transfers between devices  16 us (31%)
  Pallas kernels  6.9 us (13%)
    all_to_all x1, waiting for transfers between devices, per_device(): pieces = lax.all_to_all(total, ('yk', 'xh'), 0, 0)  13.8 us
    ppermute x3, starting transfers between devices, to_core(): lax.ppermute(a, AXES, pairs(shape, lambda y, x, c, m: (y, x, 1 - c, m)))  10.2 us
    all_to_all x1, starting transfers between devices, per_device(): pieces = lax.all_to_all(total, ('yk', 'xh'), 0, 0)  8.84 us
    ppermute x1, starting transfers between devices, to_y(): return lax.ppermute(a, AXES, pairs(shape, move))  5.09 us
    pallas_call x1, Pallas kernels, leading(): pl.pallas_call(leading_kernel, out_shape=(pltpu.VMEM(blocks, BF16), pltpu...  2.62 us
    ppermute x1, starting transfers between devices, per_device(): near = lax.ppermute(half, AXES, lower)  2.46 us
    pallas_call x1, Pallas kernels, trailing(): pl.pallas_call(trailing_kernel, out_shape=(pltpu.VMEM(blocks, BF16), pltp...  2.29 us
    ppermute x3, waiting for transfers between devices, to_core(): lax.ppermute(a, AXES, pairs(shape, lambda y, x, c, m: (y, x, 1 - c, m)))  2.23 us
  transfers between devices with their start and end apart: 7, of which 3 were waited for; matrix products, arithmetic and copies ran while one was open for 0% of the time, Pallas kernels for 7%

profile of v9, /device:TPU:199, one launch (start us, length us, event | category | flops | bytes accessed | tf_op | source)
XLA Modules:
  0.0 50.9 jit_solution(458302339812476957)
XLA Ops:
  0.0 2.6 %shard_map.46 = (bf16[8,128,256]{2,1,0:T(8,128)(2,1)S(1)}, f32[8,128,256]{2,1,0:T(8,128)S(1)}, bf16[256,512]{1,0:T(8,128)(2,1)S(1)}, bf16[256,128]{1,0:T(8,128)(2,1)S(1)}) custom-call(s32[1]{0:T(128)} %bitcast.core_ref, s32[1]{0:T(128)} %bitcast.1.parity_ref, bf16[512,256]{1,0:T(8,128)(2,1)} %grads_hbm.1, bf16[256,256]{1,0:T(8,128)(2,1)} %left_hbm.1, ...), custom_call_target="tpu_custom_call" | custom-call | flops 536870912 | bytes 2097152 | tf_op jit(solution)/shard_map/pallas_call | solution.py:126
  2.6 2.6 %collective-permute-start = (bf16[8,128,256]{2,1,0:T(8,128)(2,1)S(1)}, bf16[8,128,256]{2,1,0:T(8,128)(2,1)S(1)}, u32[]{:S(2)}, u32[]{:S(2)}) collective-permute-start(bf16[8,128,256]{2,1,0:T(8,128)(2,1)S(1)} %get-tuple-element.16), channel_id=1, source_target_pairs={{0,16},{1,17},{2,18},{3,19},{4,20},{5,21},{6,22},{7,23},{8,24},{9,... | collective-permute-start | bytes 1572872 | tf_op jit(solution)/shard_map/ppermute | solution.py:277
  5.2 1.5 %collective-permute-done.got_ref = bf16[8,128,256]{2,1,0:T(8,128)(2,1)S(1)} collective-permute-done((bf16[8,128,256]{2,1,0:T(8,128)(2,1)S(1)}, bf16[8,128,256]{2,1,0:T(8,128)(2,1)S(1)}, u32[]{:S(2)}, u32[]{:S(2)}) %collective-permute-start) | collective-permute-done | bytes 524320 | tf_op jit(solution)/shard_map/ppermute | solution.py:277
  6.7 0.1 shard_map.47
  6.8 5.1 %collective-permute-start.1 = (bf16[8,128,256]{2,1,0:T(8,128)(2,1)S(1)}, bf16[8,128,256]{2,1,0:T(8,128)(2,1)S(1)}, u32[]{:S(2)}, u32[]{:S(2)}) collective-permute-start(bf16[8,128,256]{2,1,0:T(8,128)(2,1)S(1)} %shard_map.47), channel_id=1, source_target_pairs={{0,64},{1,65},{2,66},{3,67},{4,68},{5,69},{6,70},{7,71},{8,72},{9,... | collective-permute-start | bytes 1572872 | tf_op jit(solution)/shard_map/ppermute | solution.py:283
  11.9 2.3 %shard_map.48 = (bf16[8,128,256]{2,1,0:T(8,128)(2,1)S(1)}, f32[8,128,256]{2,1,0:T(8,128)S(1)}) custom-call(s32[1]{0:T(128)} %bitcast.1.parity_ref, bf16[256,512]{1,0:T(8,128)(2,1)S(1)} %get-tuple-element.18.turned, bf16[512,4096]{1,0:T(8,128)(2,1)} %act_hbm.3), custom_call_target="tpu_custom_call" | custom-call | flops 536870912 | bytes 2097152 | tf_op jit(solution)/shard_map/pallas_call | solution.py:150
  14.2 1.9 %collective-permute-start.2 = (bf16[8,128,256]{2,1,0:T(8,128)(2,1)S(1)}, bf16[8,128,256]{2,1,0:T(8,128)(2,1)S(1)}, u32[]{:S(2)}, u32[]{:S(2)}) collective-permute-start(bf16[8,128,256]{2,1,0:T(8,128)(2,1)S(1)} %get-tuple-element.21), channel_id=1, source_target_pairs={{0,16},{1,17},{2,18},{3,19},{4,20},{5,21},{6,22},{7,23},{8,24},{9,... | collective-permute-start | bytes 1572872 | tf_op jit(solution)/shard_map/ppermute | solution.py:277
  16.2 2.5 %collective-permute-start.3 = (bf16[256,128]{1,0:T(8,128)(2,1)S(1)}, bf16[256,128]{1,0:T(8,128)(2,1)S(1)}, u32[]{:S(2)}, u32[]{:S(2)}) collective-permute-start(bf16[256,128]{1,0:T(8,128)(2,1)S(1)} %get-tuple-element.24), channel_id=1, source_target_pairs={{3,104},{12,394},{13,419},{14,457},{15,482},{20,146},{22,209},{23,... | collective-permute-start | bytes 196616 | tf_op jit(solution)/shard_map/ppermute | solution.py:288
  18.6 0.0 collective-permute-done.1.block_ref
  18.7 0.0 collective-permute-done.2.got_ref
  18.7 0.9 %shard_map.50 = bf16[8,128,256]{2,1,0:T(8,128)(2,1)} custom-call(f32[8,128,256]{2,1,0:T(8,128)S(1)} %get-tuple-element.19.keep_ref, bf16[8,128,256]{2,1,0:T(8,128)(2,1)S(1)} %shard_map.49.more_ref, bf16[8,128,256]{2,1,0:T(8,128)(2,1)S(1)} %collective-permute-done.2.got_ref), custom_call_target="tpu_custom_call" | custom-call | tf_op jit(solution)/shard_map/pallas_call | solution.py:191
  19.6 8.8 %all-to-all-start = ((bf16[8,128,256]{2,1,0:T(8,128)(2,1)}), bf16[8,128,256]{2,1,0:T(8,128)(2,1)S(1)}, u32[]{:S(2)}, u32[]{:S(2)}) async-start(bf16[8,128,256]{2,1,0:T(8,128)(2,1)} %shard_map.50), calls=%async_computation | async-start | bytes 1048576 | tf_op jit(solution)/shard_map/all_to_all | solution.py:295
  28.4 0.0 collective-permute-done.3.block_ref
  28.4 1.3 %collective-permute-start.4 = (bf16[256,128]{1,0:T(8,128)(2,1)S(1)}, bf16[256,128]{1,0:T(8,128)(2,1)S(1)}, u32[]{:S(2)}, u32[]{:S(2)}) collective-permute-start(bf16[256,128]{1,0:T(8,128)(2,1)S(1)} %get-tuple-element.24), channel_id=1, source_target_pairs={{0,0},{1,41},{2,71},{4,134},{5,175},{6,197},{7,238},{8,268},{9,293... | collective-permute-start | bytes 196616 | tf_op jit(solution)/shard_map/ppermute | solution.py:294
  29.7 13.8 %all-to-all-done.pieces_ref = bf16[8,128,256]{2,1,0:T(8,128)(2,1)S(1)} async-done(((bf16[8,128,256]{2,1,0:T(8,128)(2,1)}), bf16[8,128,256]{2,1,0:T(8,128)(2,1)S(1)}, u32[]{:S(2)}, u32[]{:S(2)}) %all-to-all-start) | async-done | bytes 524320 | tf_op jit(solution)/shard_map/all_to_all | solution.py:295
  43.5 0.1 shard_map.52.own_ref
  43.6 5.7 %collective-permute-start.5 = (bf16[128,256]{1,0:T(8,128)(2,1)S(1)}, bf16[128,256]{1,0:T(8,128)(2,1)S(1)}, u32[]{:S(2)}, u32[]{:S(2)}) collective-permute-start(bf16[128,256]{1,0:T(8,128)(2,1)S(1)} %shard_map.52.own_ref), channel_id=1, source_target_pairs={{0,16},{1,17},{2,18},{3,19},{4,20},{5,21},{6,22},{7,23},{8,24},{9,... | collective-permute-start | bytes 196616 | tf_op jit(solution)/shard_map/ppermute | solution.py:277
  49.3 0.0 collective-permute-done.4.far_ref
  49.3 0.1 shard_map.53.done_ref
  49.4 0.7 %collective-permute-done.5.other_ref = bf16[128,256]{1,0:T(8,128)(2,1)S(1)} collective-permute-done((bf16[128,256]{1,0:T(8,128)(2,1)S(1)}, bf16[128,256]{1,0:T(8,128)(2,1)S(1)}, u32[]{:S(2)}, u32[]{:S(2)}) %collective-permute-start.5) | collective-permute-done | bytes 65568 | tf_op jit(solution)/shard_map/ppermute | solution.py:277
  50.2 0.8 %shard_map.54 = bf16[256,128]{1,0:T(8,128)(2,1)} custom-call(s32[1]{0:T(128)} %bitcast.core_ref, bf16[128,128]{1,0:T(8,128)(2,1)S(1)} %shard_map.53.done_ref, bf16[128,256]{1,0:T(8,128)(2,1)S(1)} %collective-permute-done.5.other_ref, bf16[256,128]{1,0:T(8,128)(2,1)S(1)} %shard_map.51._.near_ref, bf16[256,128]{1,0:T(8,128)(2,1)S(1)} %collective-permute-done.4.far_ref), custom_call_target="tpu_custom_call" | custom-call | tf_op jit(solution)/shard_map/pallas_call | solution.py:246
  (2 shorter events, 0.0 us)
Async XLA Ops:
  2.6 4.1 %collective-permute-start = (bf16[8,128,256]{2,1,0:T(8,128)(2,1)S(1)}, bf16[8,128,256]{2,1,0:T(8,128)(2,1)S(1)}, u32[]{:S(2)}, u32[]{:S(2)}) collective-permute-start(bf16[8,128,256]{2,1,0:T(8,128)(2,1)S(1)} %get-tuple-element.16), channel_id=1, source_target_pairs={{0,16},{1,17},{2,18},{3,19},{4,20},{5,21},{6,22},{7,23},{8,24},{9,... | collective-permute-start | bytes 1572872 | tf_op jit(solution)/shard_map/ppermute | solution.py:277
  6.8 11.8 %collective-permute-start.1 = (bf16[8,128,256]{2,1,0:T(8,128)(2,1)S(1)}, bf16[8,128,256]{2,1,0:T(8,128)(2,1)S(1)}, u32[]{:S(2)}, u32[]{:S(2)}) collective-permute-start(bf16[8,128,256]{2,1,0:T(8,128)(2,1)S(1)} %shard_map.47), channel_id=1, source_target_pairs={{0,64},{1,65},{2,66},{3,67},{4,68},{5,69},{6,70},{7,71},{8,72},{9,... | collective-permute-start | bytes 1572872 | tf_op jit(solution)/shard_map/ppermute | solution.py:283
  14.2 4.4 %collective-permute-start.2 = (bf16[8,128,256]{2,1,0:T(8,128)(2,1)S(1)}, bf16[8,128,256]{2,1,0:T(8,128)(2,1)S(1)}, u32[]{:S(2)}, u32[]{:S(2)}) collective-permute-start(bf16[8,128,256]{2,1,0:T(8,128)(2,1)S(1)} %get-tuple-element.21), channel_id=1, source_target_pairs={{0,16},{1,17},{2,18},{3,19},{4,20},{5,21},{6,22},{7,23},{8,24},{9,... | collective-permute-start | bytes 1572872 | tf_op jit(solution)/shard_map/ppermute | solution.py:277
  16.2 12.3 %collective-permute-start.3 = (bf16[256,128]{1,0:T(8,128)(2,1)S(1)}, bf16[256,128]{1,0:T(8,128)(2,1)S(1)}, u32[]{:S(2)}, u32[]{:S(2)}) collective-permute-start(bf16[256,128]{1,0:T(8,128)(2,1)S(1)} %get-tuple-element.24), channel_id=1, source_target_pairs={{3,104},{12,394},{13,419},{14,457},{15,482},{20,146},{22,209},{23,... | collective-permute-start | bytes 196616 | tf_op jit(solution)/shard_map/ppermute | solution.py:288
  19.6 23.9 %all-to-all-start = ((bf16[8,128,256]{2,1,0:T(8,128)(2,1)}), bf16[8,128,256]{2,1,0:T(8,128)(2,1)S(1)}, u32[]{:S(2)}, u32[]{:S(2)}) async-start(bf16[8,128,256]{2,1,0:T(8,128)(2,1)} %shard_map.50), calls=%async_computation | async-start | bytes 1048576 | tf_op jit(solution)/shard_map/all_to_all | solution.py:295
  28.4 20.9 %collective-permute-start.4 = (bf16[256,128]{1,0:T(8,128)(2,1)S(1)}, bf16[256,128]{1,0:T(8,128)(2,1)S(1)}, u32[]{:S(2)}, u32[]{:S(2)}) collective-permute-start(bf16[256,128]{1,0:T(8,128)(2,1)S(1)} %get-tuple-element.24), channel_id=1, source_target_pairs={{0,0},{1,41},{2,71},{4,134},{5,175},{6,197},{7,238},{8,268},{9,293... | collective-permute-start | bytes 196616 | tf_op jit(solution)/shard_map/ppermute | solution.py:294
  43.6 6.6 %collective-permute-start.5 = (bf16[128,256]{1,0:T(8,128)(2,1)S(1)}, bf16[128,256]{1,0:T(8,128)(2,1)S(1)}, u32[]{:S(2)}, u32[]{:S(2)}) collective-permute-start(bf16[128,256]{1,0:T(8,128)(2,1)S(1)} %shard_map.52.own_ref), channel_id=1, source_target_pairs={{0,16},{1,17},{2,18},{3,19},{4,20},{5,21},{6,22},{7,23},{8,24},{9,... | collective-permute-start | bytes 196616 | tf_op jit(solution)/shard_map/ppermute | solution.py:277
